TPU v7x, 256 devices: a whole 4x4x8 slice. The times are simulated.
256 devices in a mesh: row: 8 (over y_hi, x), col: 32 (over y_lo, z, core).
Axes of the slice: x: 4, y: 4 (y_hi: 2, y_lo: 2; y = y_hi * 2 + y_lo), z: 8, core: 2. Of those that a mesh axis runs over, the one named last changes fastest.
Arguments:
- layer_input: bfloat16 [1024, 12288], P(('row', 'col')), may hold values from -6 to 6
- grad_y: bfloat16 [1024, 12288], P(('row', 'col')), may hold values from -6 to 6
- norm_gain: float32 [12288], replicated, may hold values from 0.25 to 1.75
- up_bias: float32 [49152], P('col'), may hold values from -3 to 3
- up_tiles: bfloat16 [384, 8, 128, 128], P('col', 'row'), may hold values from -0.1875 to 0.1875
- down_tiles: bfloat16 [384, 8, 128, 128], P('col', 'row'), may hold values from -1 to 1
- block_cols: int32 [384, 8], P('col'), may hold values from 0 to 95, as said below
- block_count: int32 [384], P('col'), may hold values from 1 to 8
Outputs:
- layer_output: bfloat16 [1024, 12288], P(('row', 'col'))
- grad_x: bfloat16 [1024, 12288], P(('row', 'col'))
- grad_gain: float32 [12288], replicated
- grad_bias: float32 [49152], P('col')
- grad_up: float32 [384, 8, 128, 128], P('col', 'row')
- grad_down: float32 [384, 8, 128, 128], P('col', 'row')
Inputs may be any that keep to these rules, and one draw needn't show every extreme that they name: `block_cols`: row i names the width blocks of the nonzero tiles of hidden block i: entries k < block_count[i] are distinct, later entries repeat entry 0.
All inputs are finite; a program needn't handle non-finite values.
Results may differ from a plain program's by a relative error of at most 0.022.
Values may be sent and summed in bfloat16 or wider, within the bound.
No kernel may reach another device: no remote copies, remote signals or barrier semaphores. Data moves between devices by JAX's collectives and lax.ppermute only.
A program may use at most 128 MiB of HBM per device.

v0:
```python
import math

import jax
import jax.numpy as jnp
from jax import lax
from jax.experimental import pallas as pl
from jax.experimental.pallas import tpu as pltpu
from jax.sharding import Mesh
from jax.sharding import PartitionSpec as P

D = 12288
HALF = D // 2
BS = 128
KMAX = 8
HID = 12
ROWS = 128
STRIP = 16

NORM_EPS = 1e-05
GELU_COEF = math.sqrt(2.0 / math.pi)
CUBIC_COEF = 0.044715
F32 = jnp.float32
BF16 = jnp.bfloat16


def shift(value, axis, steps):
    count = lax.axis_size(axis)
    return lax.ppermute(value, axis, [(i, (i + steps) % count) for i in range(count)])


def swap(value, axis, bit):
    count = lax.axis_size(axis)
    return lax.ppermute(value, axis, [(i, i ^ bit) for i in range(count)])


def step_x(value, sign):
    n, cores = lax.axis_size("x"), lax.axis_size("c")
    pairs = [
        (i * cores + c, (i + (sign if c == 0 else -sign)) % n * cores + c)
        for i in range(n)
        for c in range(cores)
    ]
    return lax.ppermute(value, ("x", "c"), pairs)


def dot(a, b, contract):
    return lax.dot_general(a, b, (contract, ((), ())), preferred_element_type=F32)


def compute_kernel(*refs):
    cols, core = refs[:2]
    tiles = refs[2:8]
    bias, gain = refs[8:10]
    near, far = refs[10:19], refs[19:28]
    keep = refs[28:36]
    send_last, send_rest = refs[36:38]
    grads = refs[38:44]
    bias_sum, gain_sum = refs[44:46]
    x_all, dy_all, out_acc, in_acc, sems = refs[46:]

    mine = pl.multiple_of(core[0] * HALF, BS)
    other = pl.multiple_of((1 - core[0]) * HALF, BS)
    copies = []
    for pieces, start in ((near, mine), (far, other)):
        for which, target in ((0, x_all), (1, dy_all)):
            for j in range(8):
                source = pieces[j].at[which] if j < 7 else pieces[7 + which]
                copies.append(
                    pltpu.make_async_copy(
                        source,
                        target.at[pl.ds(j * STRIP, STRIP), pl.ds(start, HALF)],
                        sems.at[len(copies)],
                    )
                )
    for copy in copies:
        copy.start()
    out_acc[...] = jnp.zeros_like(out_acc)
    in_acc[...] = jnp.zeros_like(in_acc)
    for copy in copies:
        copy.wait()

    which = (0, 1, 2, 3, 4, 4, 5, 5)
    first = (0, 0, 0, 0, 0, 2 * HID, 0, 2 * HID)

    def hidden_block(i, carry):
        spans = [pl.ds(pl.multiple_of(cols[i, p] * BS, BS), BS) for p in range(KMAX)]
        x_pick = jnp.concatenate([x_all[:, s] for s in spans], axis=1)
        dy_pick = jnp.concatenate([dy_all[:, s] for s in spans], axis=1)
        up = jnp.concatenate([tiles[which[p]][first[p] + i] for p in range(KMAX)], axis=0)
        down = jnp.concatenate(
            [tiles[which[p]][first[p] + HID + i] for p in range(KMAX)], axis=1
        )
        hidden = dot(x_pick, up, ((1,), (0,))) + bias[i]
        act_grad = dot(dy_pick, down, ((1,), (1,)))
        squared = hidden * hidden
        bent = jnp.tanh(GELU_COEF * (hidden + CUBIC_COEF * squared * hidden))
        activated = (0.5 * hidden * (1.0 + bent)).astype(BF16)
        slope = 0.5 * (1.0 + bent) + 0.5 * hidden * (1.0 - bent * bent) * GELU_COEF * (
            1.0 + 3.0 * CUBIC_COEF * squared
        )
        hidden_full = act_grad * slope
        bias_sum[i] = jnp.sum(hidden_full, axis=0, keepdims=True)
        hidden_grad = hidden_full.astype(BF16)
        contrib = dot(activated, down, ((1,), (0,)))
        for p in range(KMAX):
            out_acc[:, spans[p]] += contrib[:, p * BS : (p + 1) * BS]
        down_grad = dot(activated, dy_pick, ((0,), (0,))).astype(BF16)
        back = dot(hidden_grad, up, ((1,), (1,)))
        for p in range(KMAX):
            in_acc[:, spans[p]] += back[:, p * BS : (p + 1) * BS]
        up_grad = dot(x_pick, hidden_grad, ((0,), (0,))).astype(BF16)
        for p in range(KMAX):
            grads[which[p]][first[p] + i] = up_grad[p * BS : (p + 1) * BS]
            grads[which[p]][first[p] + HID + i] = down_grad[:, p * BS : (p + 1) * BS]
        return carry

    lax.fori_loop(0, HID, hidden_block, 0)

    for j in range(8):
        rows = pl.ds(j * STRIP, STRIP)
        for part, acc in ((0, out_acc), (1, in_acc)):
            keep[j][part] = acc[rows, pl.ds(mine, HALF)].astype(BF16)
            target = send_last.at[part] if j == 7 else send_rest.at[j, part]
            target[...] = acc[rows, pl.ds(other, HALF)].astype(BF16)

    def gain_strip(b, carry):
        span = pl.ds(pl.multiple_of(b * 4 * BS, BS), 4 * BS)
        total = jnp.sum(in_acc[:, span] * x_all[:, span].astype(F32), axis=0, keepdims=True)
        gain_sum[:, span] = total / gain[:, span]
        return carry

    lax.fori_loop(0, D // (4 * BS), gain_strip, 0)


def compute(cols, core, tiles, bias, gain, near, far):
    vmem = pl.BlockSpec(memory_space=pltpu.VMEM)
    smem = pl.BlockSpec(memory_space=pltpu.SMEM)
    anyspace = pl.BlockSpec(memory_space=pl.ANY)
    part = jax.ShapeDtypeStruct((2, STRIP, HALF), BF16)
    out_shape = (
        [part] * 9
        + [jax.ShapeDtypeStruct((7, 2, STRIP, HALF), BF16)]
        + [jax.ShapeDtypeStruct(t.shape, BF16) for t in tiles]
        + [jax.ShapeDtypeStruct((HID, 1, BS), F32), jax.ShapeDtypeStruct((1, D), F32)]
    )
    outs = pl.pallas_call(
        compute_kernel,
        out_shape=out_shape,
        in_specs=[smem, smem] + [vmem] * 8 + [anyspace] * 18,
        out_specs=[vmem] * len(out_shape),
        scratch_shapes=[
            pltpu.VMEM((ROWS, D), BF16),
            pltpu.VMEM((ROWS, D), BF16),
            pltpu.VMEM((ROWS, D), F32),
            pltpu.VMEM((ROWS, D), F32),
            pltpu.SemaphoreType.DMA((32,)),
        ],
        compiler_params=pltpu.CompilerParams(vmem_limit_bytes=50 * 1024 * 1024),
        cost_estimate=pl.CostEstimate(
            flops=2_400_000_000, bytes_accessed=25_000_000, transcendentals=200_000
        ),
        name="butterfly_ffn",
    )(cols, core, *tiles, bias, gain, *near, *far)
    return outs[:8], outs[8], outs[9], outs[10:16], outs[16], outs[17]


def add(a, b):
    return (a.astype(F32) + b.astype(F32)).astype(BF16)


def add3(*values):
    return sum(v.astype(F32) for v in values)


def together(*values):
    return lax.optimization_barrier(values)


def on_device(layer_input, grad_y, norm_gain, up_bias, up_tiles, down_tiles, block_cols, block_count):
    core = lax.axis_index("c")
    xi, yh = lax.axis_index("x"), lax.axis_index("yh")
    n_x = lax.axis_size("x")
    is_first = core == 0

    kept = (yh * n_x + xi < block_count).astype(BF16)[:, None, None]
    near_t = jnp.concatenate([up_tiles[:, 0] * kept, down_tiles[:, 0] * kept], axis=0)
    across = (xi + 2) % n_x
    odd = jnp.where(is_first, xi - 1, xi + 1) % n_x
    odd_across = (odd + 2) % n_x
    near_y, far_y = yh * n_x, (1 - yh) * n_x
    slots = jnp.stack(
        [near_y + xi, far_y + xi, near_y + across, far_y + across]
        + [near_y + odd, near_y + odd_across, far_y + odd, far_y + odd_across]
    )
    cols = jnp.take(block_cols, slots, axis=1)

    x_float = layer_input.astype(F32)
    norm_factor = lax.rsqrt(jnp.mean(x_float * x_float, axis=-1, keepdims=True) + NORM_EPS)
    x_unit = x_float * norm_factor
    normed = (x_unit * norm_gain[None, :]).astype(BF16)
    own = jnp.stack([normed, grad_y])
    low, high = own[:, :, :HALF], own[:, :, HALF:]
    mine, theirs = jnp.where(is_first, low, high), jnp.where(is_first, high, low)

    near2_t = swap(near_t, "x", 2)
    far_t = swap(near_t, "yh", 1)
    came = swap(theirs, "c", 1)
    pair = jnp.concatenate(
        [jnp.where(is_first, mine, came), jnp.where(is_first, came, mine)], axis=1
    )
    piece = jnp.concatenate([pair, swap(pair, "yl", 1)], axis=1)
    r1, l1 = shift(piece, "z", 1), shift(piece, "z", -1)
    near2_t, far_t, r1, l1 = together(near2_t, far_t, r1, l1)
    near_odd = step_x(jnp.concatenate([near_t, near2_t], axis=0), 1)
    far2_t = swap(near2_t, "yh", 1)
    r2, l2 = shift(r1, "z", 1), shift(l1, "z", -1)
    c_piece, c_r1, c_l1 = [swap(p, "c", 1) for p in (piece, r1, l1)]
    r3, l3 = shift(r2, "z", 1), shift(l2, "z", -1)
    far2_t, near_odd, r3, l3, c_piece, c_r1, c_l1 = together(
        far2_t, near_odd, r3, l3, c_piece, c_r1, c_l1
    )
    far_odd = step_x(jnp.concatenate([far_t, far2_t], axis=0), 1)
    x4, dy4 = shift(r3[0], "z", 1), shift(l3[1], "z", -1)
    c_r2, c_l2, c_r3, c_l3, c_x4, c_dy4 = [swap(p, "c", 1) for p in (r2, l2, r3, l3, x4, dy4)]
    near = [piece, r1, r2, r3, l1, l2, l3, x4, dy4]
    far = [c_piece, c_r1, c_r2, c_r3, c_l1, c_l2, c_l3, c_x4, c_dy4]

    keep, send_last, send_rest, grads, bias_part, gain_part = compute(
        cols,
        core.reshape(1),
        [near_t, far_t, near2_t, far2_t, near_odd, far_odd],
        up_bias.reshape(HID, 1, BS),
        norm_gain[None, :],
        near,
        far,
    )
    g_n, g_f, g_n2, g_f2, g_no, g_fo = grads
    sums = jnp.concatenate([gain_part[0], bias_part.reshape(HID * BS)])
    p0, m1, m2, m3, q1, q2, q3, p4 = keep

    last = swap(send_last, "c", 1)
    rest = swap(send_rest, "c", 1)
    sums = sums + swap(sums, "x", 1)
    came_s = swap(sums, "x", 2)
    came_s, last, g_fo, g_no = together(came_s, last, g_fo, g_no)
    from_fo, from_no = step_x(g_fo, -1), step_x(g_no, -1)
    sums = sums + came_s
    p4 = add(p4, last)
    up_half, down_half = shift(p4[0], "z", 1), shift(p4[1], "z", -1)
    came_s = swap(sums, "yh", 1)
    up_half, down_half, came_s, rest = together(up_half, down_half, came_s, rest)
    sums = sums + came_s
    grad_bias, grad_gain = sums[D:], sums[:D]
    q3, m3 = add3(q3, rest[6]), add3(m3, rest[3])
    q3 = jnp.stack([q3[0] + up_half.astype(F32), q3[1]]).astype(BF16)
    m3 = jnp.stack([m3[0], m3[1] + down_half.astype(F32)]).astype(BF16)
    up3, down3 = shift(q3, "z", 1), shift(m3, "z", -1)
    came_s = swap(grad_gain, "yl", 1)
    up3, down3, came_s, from_fo = together(up3, down3, came_s, from_fo)
    g_f2 = add(g_f2, from_fo[2 * HID :])
    from_f2 = swap(g_f2, "yh", 1)
    grad_gain = grad_gain + came_s
    q2, m2 = add3(q2, rest[5], up3).astype(BF16), add3(m2, rest[2], down3).astype(BF16)
    up2, down2 = shift(q2, "z", 1), shift(m2, "z", -1)
    came_s = swap(grad_gain, "z", 1)
    g_f = add(g_f, from_fo[: 2 * HID])
    up2, down2, came_s, from_no, from_f2, g_f = together(
        up2, down2, came_s, from_no, from_f2, g_f
    )
    g_n2 = add3(g_n2, from_no[2 * HID :], from_f2).astype(BF16)
    from_n2 = swap(g_n2, "x", 2)
    from_f = swap(g_f, "yh", 1)
    grad_gain = grad_gain + came_s
    q1, m1 = add3(q1, rest[4], up2).astype(BF16), add3(m1, rest[1], down2).astype(BF16)
    up1, down1 = shift(q1, "z", 1), shift(m1, "z", -1)
    came_s = swap(grad_gain, "z", 2)
    up1, down1, came_s = together(up1, down1, came_s)
    grad_gain = grad_gain + came_s
    total = add3(p0, rest[0], up1, down1)
    eight = STRIP // 2
    came_y = swap(total[:, eight:].astype(BF16), "yl", 1)
    came_s = swap(grad_gain, "z", 4)
    came_y, came_s, from_n2, from_f = together(came_y, came_s, from_n2, from_f)
    grad_gain = grad_gain + came_s
    total = total[:, :eight] + came_y.astype(F32)
    four = eight // 2
    mine_t = jnp.where(is_first, total[:, :four], total[:, four:])
    send_t = jnp.where(is_first, total[:, four:], total[:, :four]).astype(BF16)
    came_t = swap(send_t, "c", 1).astype(F32)
    grad_gain = grad_gain + swap(grad_gain, "c", 1)
    both = jnp.concatenate(
        [jnp.where(is_first, mine_t, came_t), jnp.where(is_first, came_t, mine_t)], axis=2
    )
    layer_output = (x_float + both[0]).astype(BF16)
    normed_grad = both[1]
    scaled = normed_grad * norm_gain[None, :]
    inner = jnp.mean(scaled * x_unit, axis=-1, keepdims=True)
    grad_x = (grad_y.astype(F32) + norm_factor * (scaled - x_unit * inner)).astype(BF16)
    g_own = add3(g_n, from_no[: 2 * HID], from_n2, from_f)
    kept_f = kept.astype(F32)
    grad_up = (g_own[:HID] * kept_f)[:, None]
    grad_down = (g_own[HID:] * kept_f)[:, None]
    return (layer_output, grad_x, grad_gain, grad_bias, grad_up, grad_down)


def solution(mesh):
    fine = Mesh(mesh.devices.reshape(2, 4, 2, 8, 2), ("yh", "x", "yl", "z", "c"))
    row, col = ("yh", "x"), ("yl", "z", "c")
    tokens = P(row + col, None)
    tiles = P(col, row, None, None)
    return jax.shard_map(
        on_device,
        mesh=fine,
        in_specs=(tokens, tokens, P(), P(col), tiles, tiles, P(col, None), P(col)),
        out_specs=(tokens, tokens, P(), P(col), tiles, tiles),
        check_vma=False,
    )
```

profile of v0, /device:TPU:41, one launch (start us, length us, event | category | flops | bytes accessed | tf_op | source)
XLA Modules:
  0.0 201.5 jit_solution(6092665436440521636)
XLA Ops:
  0.7 1.2 fusion.25
  1.9 1.0 fusion.34
  2.9 0.9 broadcast_select_fusion.2
  3.8 0.8 collective-permute-start.2
  4.6 0.7 fusion.37
  5.5 1.1 broadcast_select_fusion.1
  7.2 2.4 %collective-permute-start.1 = (bf16[24,128,128]{2,1,0:T(8,128)(2,1)S(1)}, bf16[24,128,128]{2,1,0:T(8,128)(2,1)S(1)}, u32[]{:S(2)}, u32[]{:S(2)}) collective-permute-start(bf16[24,128,128]{2,1,0:T(8,128)(2,1)S(1)} %pad_maximum_fusion.2.refs_2_), channel_id=1, source_target_pairs={{0,128},{128,0},{1,129},{129,1},{2,130},{130,2},{3,131},{131,3},{4... | collective-permute-start | bytes 2359304 | tf_op jit(solution)/shard_map/ppermute | solution.py:33
  9.6 2.7 %collective-permute-start = (bf16[24,128,128]{2,1,0:T(8,128)(2,1)S(1)}, bf16[24,128,128]{2,1,0:T(8,128)(2,1)S(1)}, u32[]{:S(2)}, u32[]{:S(2)}) collective-permute-start(bf16[24,128,128]{2,1,0:T(8,128)(2,1)S(1)} %pad_maximum_fusion.2.refs_2_), channel_id=1, source_target_pairs={{0,64},{32,96},{64,0},{96,32},{1,65},{33,97},{65,1},{97,33},{2,66}... | collective-permute-start | bytes 2359304 | tf_op jit(solution)/shard_map/ppermute | solution.py:33
  12.3 0.6 collective-permute-done.3
  13.1 0.7 collective-permute-start.5
  13.8 1.1 collective-permute-start.4
  14.9 7.4 %collective-permute-done.5.refs_14_ = bf16[2,16,6144]{2,1,0:T(8,128)(2,1)} collective-permute-done((bf16[2,16,6144]{2,1,0:T(8,128)(2,1)S(1)}, bf16[2,16,6144]{2,1,0:T(8,128)(2,1)}, u32[]{:S(2)}, u32[]{:S(2)}) %collective-permute-start.5) | collective-permute-done | bytes 393248 | tf_op jit(solution)/shard_map/ppermute | solution.py:28
  22.3 3.5 %collective-permute-done.4.refs_11_ = bf16[2,16,6144]{2,1,0:T(8,128)(2,1)S(1)} collective-permute-done((bf16[2,16,6144]{2,1,0:T(8,128)(2,1)S(1)}, bf16[2,16,6144]{2,1,0:T(8,128)(2,1)S(1)}, u32[]{:S(2)}, u32[]{:S(2)}) %collective-permute-start.4) | collective-permute-done | bytes 393248 | tf_op jit(solution)/shard_map/ppermute | solution.py:28
  25.7 5.0 %collective-permute-done.1.refs_3_ = bf16[24,128,128]{2,1,0:T(8,128)(2,1)S(1)} collective-permute-done((bf16[24,128,128]{2,1,0:T(8,128)(2,1)S(1)}, bf16[24,128,128]{2,1,0:T(8,128)(2,1)S(1)}, u32[]{:S(2)}, u32[]{:S(2)}) %collective-permute-start.1) | collective-permute-done | bytes 786464 | tf_op jit(solution)/shard_map/ppermute | solution.py:33
  30.8 1.5 pad_maximum_fusion
  32.2 2.5 %collective-permute-start.7 = (bf16[48,128,128]{2,1,0:T(8,128)(2,1)}, bf16[48,128,128]{2,1,0:T(8,128)(2,1)}, u32[]{:S(2)}, u32[]{:S(2)}) collective-permute-start(bf16[48,128,128]{2,1,0:T(8,128)(2,1)} %pad_maximum_fusion), channel_id=1, source_target_pairs={{0,32},{1,97},{32,64},{33,1},{64,96},{65,33},{96,0},{97,65},{2,34}... | collective-permute-start | bytes 4718600 | tf_op jit(solution)/shard_map/ppermute | solution.py:43
  35.2 1.6 collective-permute-start.8
  36.9 0.7 collective-permute-start.6
  37.6 0.8 collective-permute-start.14
  38.5 7.4 %collective-permute-done.8.refs_12_ = bf16[2,16,6144]{2,1,0:T(8,128)(2,1)} collective-permute-done((bf16[2,16,6144]{2,1,0:T(8,128)(2,1)S(1)}, bf16[2,16,6144]{2,1,0:T(8,128)(2,1)}, u32[]{:S(2)}, u32[]{:S(2)}) %collective-permute-start.8) | collective-permute-done | bytes 393248 | tf_op jit(solution)/shard_map/ppermute | solution.py:28
  45.9 1.6 collective-permute-start.9
  47.8 2.5 %collective-permute-start.11 = (bf16[2,16,6144]{2,1,0:T(8,128)(2,1)}, bf16[2,16,6144]{2,1,0:T(8,128)(2,1)S(1)}, u32[]{:S(2)}, u32[]{:S(2)}) collective-permute-start(bf16[2,16,6144]{2,1,0:T(8,128)(2,1)} %collective-permute-done.10.refs_15_), channel_id=1, source_target_pairs={{0,14},{2,0},{4,2},{6,4},{8,6},{10,8},{12,10},{14,12},{1,15},{3,1}... | collective-permute-start | bytes 1179656 | tf_op jit(solution)/shard_map/ppermute | solution.py:28
  51.1 1.1 collective-permute-start.18
  52.2 7.0 %collective-permute-done.9.refs_13_ = bf16[2,16,6144]{2,1,0:T(8,128)(2,1)S(1)} collective-permute-done((bf16[2,16,6144]{2,1,0:T(8,128)(2,1)}, bf16[2,16,6144]{2,1,0:T(8,128)(2,1)S(1)}, u32[]{:S(2)}, u32[]{:S(2)}) %collective-permute-start.9) | collective-permute-done | bytes 393248 | tf_op jit(solution)/shard_map/ppermute | solution.py:28
  59.2 1.5 collective-permute-start.20
  61.6 0.8 collective-permute-start.15
  62.9 2.4 %collective-permute-start.17 = (bf16[16,6144]{1,0:T(8,128)(2,1)S(1)}, bf16[16,6144]{1,0:T(8,128)(2,1)S(1)}, u32[]{:S(2)}, u32[]{:S(2)}) collective-permute-start(bf16[16,6144]{1,0:T(8,128)(2,1)S(1)} %slice_bitcast_fusion.4), channel_id=1, source_target_pairs={{0,14},{2,0},{4,2},{6,4},{8,6},{10,8},{12,10},{14,12},{1,15},{3,1}... | collective-permute-start | bytes 589832 | tf_op jit(solution)/shard_map/ppermute | solution.py:28
  65.6 5.0 %collective-permute-done.17.refs_18_ = bf16[16,6144]{1,0:T(8,128)(2,1)S(1)} collective-permute-done((bf16[16,6144]{1,0:T(8,128)(2,1)S(1)}, bf16[16,6144]{1,0:T(8,128)(2,1)S(1)}, u32[]{:S(2)}, u32[]{:S(2)}) %collective-permute-start.17) | collective-permute-done | bytes 196640 | tf_op jit(solution)/shard_map/ppermute | solution.py:28
  70.6 0.7 collective-permute-start.23
  71.3 1.4 collective-permute-done.16.refs_17_
  72.7 0.9 collective-permute-start.22
  73.7 1.0 collective-permute-done.22.refs_26_
  74.7 6.5 %collective-permute-done.15.refs_7_ = bf16[48,128,128]{2,1,0:T(8,128)(2,1)S(1)} collective-permute-done((bf16[48,128,128]{2,1,0:T(8,128)(2,1)S(1)}, bf16[48,128,128]{2,1,0:T(8,128)(2,1)S(1)}, u32[]{:S(2)}, u32[]{:S(2)}) %collective-permute-start.15) | collective-permute-done | bytes 1572896 | tf_op jit(solution)/shard_map/ppermute | solution.py:43
  81.2 1.1 copy-done.8
  82.3 19.6 %butterfly_ffn.1 = (bf16[2,16,6144]{2,1,0:T(8,128)(2,1)S(1)}, bf16[2,16,6144]{2,1,0:T(8,128)(2,1)S(1)}, bf16[2,16,6144]{2,1,0:T(8,128)(2,1)S(1)}, bf16[2,16,6144...) custom-call(s32[12,8]{1,0:T(8,128)S(1)} %select_bitcast_fusion.refs_, ...), custom_call_target="tpu_custom_call" | custom-call | flops 2400000000 | bytes 25000000 | tf_op jit(solution)/shard_map/butterfly_ffn/pallas_call | solution.py:146
  102.0 0.6 collective-permute-start.24
  102.6 1.9 collective-permute-start.26
  105.1 1.8 collective-permute-start.25
  106.9 2.6 %collective-permute-start.30 = (bf16[7,2,16,6144]{3,2,1,0:T(8,128)(2,1)}, bf16[7,2,16,6144]{3,2,1,0:T(8,128)(2,1)S(1)}, u32[]{:S(2)}, u32[]{:S(2)}) collective-permute-start(bf16[7,2,16,6144]{3,2,1,0:T(8,128)(2,1)} %get-tuple-element.80), channel_id=1, source_target_pairs={{0,1},{1,0},{2,3},{3,2},{4,5},{5,4},{6,7},{7,6},{8,9},{9,8},{10,11... | collective-permute-start | bytes 8257544 | tf_op jit(solution)/shard_map/ppermute | solution.py:33
  109.9 2.8 %collective-permute-start.28 = (bf16[16,6144]{1,0:T(8,128)(2,1)S(1)}, bf16[16,6144]{1,0:T(8,128)(2,1)S(1)}, u32[]{:S(2)}, u32[]{:S(2)}) collective-permute-start(bf16[16,6144]{1,0:T(8,128)(2,1)S(1)} %get-tuple-element.136), channel_id=1, source_target_pairs={{0,14},{2,0},{4,2},{6,4},{8,6},{10,8},{12,10},{14,12},{1,15},{3,1}... | collective-permute-start | bytes 589832 | tf_op jit(solution)/shard_map/ppermute | solution.py:28
  112.7 0.7 collective-permute-start.29
  113.4 11.0 %collective-permute-start.34 = (bf16[48,128,128]{2,1,0:T(8,128)(2,1)S(1)}, bf16[48,128,128]{2,1,0:T(8,128)(2,1)S(1)}, u32[]{:S(2)}, u32[]{:S(2)}) collective-permute-start(bf16[48,128,128]{2,1,0:T(8,128)(2,1)S(1)} %copy-done.27), channel_id=1, source_target_pairs={{0,96},{1,33},{32,0},{33,65},{64,32},{65,97},{96,64},{97,1},{2,98}... | collective-permute-start | bytes 4718600 | tf_op jit(solution)/shard_map/ppermute | solution.py:43
  124.7 2.7 %collective-permute-start.31 = (bf16[2,16,6144]{2,1,0:T(8,128)(2,1)S(1)}, bf16[2,16,6144]{2,1,0:T(8,128)(2,1)S(1)}, u32[]{:S(2)}, u32[]{:S(2)}) collective-permute-start(bf16[2,16,6144]{2,1,0:T(8,128)(2,1)S(1)} %pad_maximum_fusion.4), channel_id=1, source_target_pairs={{0,2},{2,4},{4,6},{6,8},{8,10},{10,12},{12,14},{14,0},{1,3},{3,5},... | collective-permute-start | bytes 1179656 | tf_op jit(solution)/shard_map/ppermute | solution.py:28
  127.7 1.4 collective-permute-start.33
  129.1 0.8 collective-permute-start.38
  129.9 13.8 %collective-permute-done.34 = bf16[48,128,128]{2,1,0:T(8,128)(2,1)S(1)} collective-permute-done((bf16[48,128,128]{2,1,0:T(8,128)(2,1)S(1)}, bf16[48,128,128]{2,1,0:T(8,128)(2,1)S(1)}, u32[]{:S(2)}, u32[]{:S(2)}) %collective-permute-start.34) | collective-permute-done | bytes 1572896 | tf_op jit(solution)/shard_map/ppermute | solution.py:43
  143.7 0.6 add_convert_fusion.1
  144.3 2.5 %collective-permute-start.39 = (bf16[24,128,128]{2,1,0:T(8,128)(2,1)S(1)}, bf16[24,128,128]{2,1,0:T(8,128)(2,1)S(1)}, u32[]{:S(2)}, u32[]{:S(2)}) collective-permute-start(bf16[24,128,128]{2,1,0:T(8,128)(2,1)S(1)} %get-tuple-element.131), channel_id=1, source_target_pairs={{0,128},{128,0},{1,129},{129,1},{2,130},{130,2},{3,131},{131,3},{4... | collective-permute-start | bytes 2359304 | tf_op jit(solution)/shard_map/ppermute | solution.py:33
  147.0 2.1 %collective-permute-start.36 = (bf16[2,16,6144]{2,1,0:T(8,128)(2,1)S(1)}, bf16[2,16,6144]{2,1,0:T(8,128)(2,1)S(1)}, u32[]{:S(2)}, u32[]{:S(2)}) collective-permute-start(bf16[2,16,6144]{2,1,0:T(8,128)(2,1)S(1)} %get-tuple-element.124), channel_id=1, source_target_pairs={{0,14},{2,0},{4,2},{6,4},{8,6},{10,8},{12,10},{14,12},{1,15},{3,1}... | collective-permute-start | bytes 1179656 | tf_op jit(solution)/shard_map/ppermute | solution.py:28
  149.7 2.2 %collective-permute-start.37 = (f32[12288]{0:T(1024)S(1)}, f32[12288]{0:T(1024)S(1)}, u32[]{:S(2)}, u32[]{:S(2)}) collective-permute-start(f32[12288]{0:T(1024)S(1)} %slice_add_fusion.1), channel_id=1, source_target_pairs={{0,2},{2,0},{4,6},{6,4},{8,10},{10,8},{12,14},{14,12},{1,3},{3,1},... | collective-permute-start | bytes 147464 | tf_op jit(solution)/shard_map/ppermute | solution.py:33
  151.9 8.8 %collective-permute-done.38 = bf16[48,128,128]{2,1,0:T(8,128)(2,1)S(1)} collective-permute-done((bf16[48,128,128]{2,1,0:T(8,128)(2,1)S(1)}, bf16[48,128,128]{2,1,0:T(8,128)(2,1)S(1)}, u32[]{:S(2)}, u32[]{:S(2)}) %collective-permute-start.38) | collective-permute-done | bytes 1572896 | tf_op jit(solution)/shard_map/ppermute | solution.py:43
  161.0 2.3 %collective-permute-start.41 = (bf16[2,16,6144]{2,1,0:T(8,128)(2,1)S(1)}, bf16[2,16,6144]{2,1,0:T(8,128)(2,1)S(1)}, u32[]{:S(2)}, u32[]{:S(2)}) collective-permute-start(bf16[2,16,6144]{2,1,0:T(8,128)(2,1)S(1)} %get-tuple-element.122), channel_id=1, source_target_pairs={{0,14},{2,0},{4,2},{6,4},{8,6},{10,8},{12,10},{14,12},{1,15},{3,1}... | collective-permute-start | bytes 1179656 | tf_op jit(solution)/shard_map/ppermute | solution.py:28
  163.7 5.0 %collective-permute-start.42 = (f32[12288]{0:T(1024)S(1)}, f32[12288]{0:T(1024)S(1)}, u32[]{:S(2)}, u32[]{:S(2)}) collective-permute-start(f32[12288]{0:T(1024)S(1)} %add.207), channel_id=1, source_target_pairs={{0,4},{2,6},{4,0},{6,2},{8,12},{10,14},{12,8},{14,10},{1,5},{3,7},... | collective-permute-start | bytes 147464 | tf_op jit(solution)/shard_map/ppermute | solution.py:33
  169.2 1.3 collective-permute-start.45
  170.4 2.3 %collective-permute-start.46 = (bf16[24,128,128]{2,1,0:T(8,128)(2,1)S(1)}, bf16[24,128,128]{2,1,0:T(8,128)(2,1)S(1)}, u32[]{:S(2)}, u32[]{:S(2)}) collective-permute-start(bf16[24,128,128]{2,1,0:T(8,128)(2,1)S(1)} %get-tuple-element.108), channel_id=1, source_target_pairs={{0,128},{128,0},{1,129},{129,1},{2,130},{130,2},{3,131},{131,3},{4... | collective-permute-start | bytes 2359304 | tf_op jit(solution)/shard_map/ppermute | solution.py:33
  173.0 1.7 collective-permute-start.43
  174.7 2.0 %collective-permute-start.44 = (f32[12288]{0:T(1024)S(1)}, f32[12288]{0:T(1024)S(1)}, u32[]{:S(2)}, u32[]{:S(2)}) collective-permute-start(f32[12288]{0:T(1024)S(1)} %add.210), channel_id=1, source_target_pairs={{0,8},{2,10},{4,12},{6,14},{8,0},{10,2},{12,4},{14,6},{1,9},{3,11}... | collective-permute-start | bytes 147464 | tf_op jit(solution)/shard_map/ppermute | solution.py:33
  176.8 0.6 slice.146
  177.4 4.2 %collective-permute-done.44 = f32[12288]{0:T(1024)S(1)} collective-permute-done((f32[12288]{0:T(1024)S(1)}, f32[12288]{0:T(1024)S(1)}, u32[]{:S(2)}, u32[]{:S(2)}) %collective-permute-start.44) | collective-permute-done | bytes 49184 | tf_op jit(solution)/shard_map/ppermute | solution.py:33
  181.6 8.2 %collective-permute-done.43 = bf16[2,8,6144]{2,1,0:T(8,128)(2,1)S(1)} collective-permute-done((bf16[2,8,6144]{2,1,0:T(8,128)(2,1)S(1)}, bf16[2,8,6144]{2,1,0:T(8,128)(2,1)S(1)}, u32[]{:S(2)}, u32[]{:S(2)}) %collective-permute-start.43) | collective-permute-done | bytes 196640 | tf_op jit(solution)/shard_map/ppermute | solution.py:33
  189.8 7.4 %collective-permute-start.48 = (f32[12288]{0:T(1024)S(1)}, f32[12288]{0:T(1024)S(1)}, u32[]{:S(2)}, u32[]{:S(2)}) collective-permute-start(f32[12288]{0:T(1024)S(1)} %add.216), channel_id=1, source_target_pairs={{0,1},{1,0},{2,3},{3,2},{4,5},{5,4},{6,7},{7,6},{8,9},{9,8},{10,11... | collective-permute-start | bytes 147464 | tf_op jit(solution)/shard_map/ppermute | solution.py:33
  197.9 1.4 fusion
  199.3 0.6 add.217
  200.4 0.9 fusion.24
  (149 shorter events, 9.1 us)
Async XLA Ops:
  0.6 49.7 %copy-start = (s32[12,8]{0,1:T(8,128)S(1)}, s32[12,8]{0,1:T(8,128)}, u32[]{:S(2)}) copy-start(s32[12,8]{0,1:T(8,128)} %param.14) | copy-start | bytes 1156
  3.8 1.7 collective-permute-start.2
  6.7 6.2 %collective-permute-start.3 = (bf16[2,8,6144]{2,1,0:T(8,128)(2,1)S(1)}, bf16[2,8,6144]{2,1,0:T(8,128)(2,1)S(1)}, u32[]{:S(2)}, u32[]{:S(2)}) collective-permute-start(bf16[2,8,6144]{2,1,0:T(8,128)(2,1)S(1)} %pad_maximum_fusion.7), channel_id=1, source_target_pairs={{0,16},{16,0},{1,17},{17,1},{2,18},{18,2},{3,19},{19,3},{4,20},{20... | collective-permute-start | bytes 589832 | tf_op jit(solution)/shard_map/ppermute | solution.py:33
  7.2 23.6 %collective-permute-start.1 = (bf16[24,128,128]{2,1,0:T(8,128)(2,1)S(1)}, bf16[24,128,128]{2,1,0:T(8,128)(2,1)S(1)}, u32[]{:S(2)}, u32[]{:S(2)}) collective-permute-start(bf16[24,128,128]{2,1,0:T(8,128)(2,1)S(1)} %pad_maximum_fusion.2.refs_2_), channel_id=1, source_target_pairs={{0,128},{128,0},{1,129},{129,1},{2,130},{130,2},{3,131},{131,3},{4... | collective-permute-start | bytes 2359304 | tf_op jit(solution)/shard_map/ppermute | solution.py:33
  9.6 21.2 %collective-permute-start = (bf16[24,128,128]{2,1,0:T(8,128)(2,1)S(1)}, bf16[24,128,128]{2,1,0:T(8,128)(2,1)S(1)}, u32[]{:S(2)}, u32[]{:S(2)}) collective-permute-start(bf16[24,128,128]{2,1,0:T(8,128)(2,1)S(1)} %pad_maximum_fusion.2.refs_2_), channel_id=1, source_target_pairs={{0,64},{32,96},{64,0},{96,32},{1,65},{33,97},{65,1},{97,33},{2,66}... | collective-permute-start | bytes 2359304 | tf_op jit(solution)/shard_map/ppermute | solution.py:33
  13.1 21.7 %copy-start.6 = (bf16[2,16,6144]{2,1,0:T(8,128)(2,1)}, bf16[2,16,6144]{2,1,0:T(8,128)(2,1)S(1)}, u32[]{:S(2)}) copy-start(bf16[2,16,6144]{2,1,0:T(8,128)(2,1)S(1)} %pad_maximum_fusion.3.refs_10_) | copy-start | bytes 1179652
  13.1 37.9 %copy-start.25 = (f32[1536]{0:T(1024)S(1)}, f32[1536]{0:T(1024)}, u32[]{:S(2)}) copy-start(f32[1536]{0:T(1024)} %param.11) | copy-start | bytes 18436
  13.1 9.2 %collective-permute-start.5 = (bf16[2,16,6144]{2,1,0:T(8,128)(2,1)S(1)}, bf16[2,16,6144]{2,1,0:T(8,128)(2,1)}, u32[]{:S(2)}, u32[]{:S(2)}) collective-permute-start(bf16[2,16,6144]{2,1,0:T(8,128)(2,1)S(1)} %pad_maximum_fusion.3.refs_10_), channel_id=1, source_target_pairs={{0,14},{2,0},{4,2},{6,4},{8,6},{10,8},{12,10},{14,12},{1,15},{3,1}... | collective-permute-start | bytes 1179656 | tf_op jit(solution)/shard_map/ppermute | solution.py:28
  13.8 12.0 %collective-permute-start.4 = (bf16[2,16,6144]{2,1,0:T(8,128)(2,1)S(1)}, bf16[2,16,6144]{2,1,0:T(8,128)(2,1)S(1)}, u32[]{:S(2)}, u32[]{:S(2)}) collective-permute-start(bf16[2,16,6144]{2,1,0:T(8,128)(2,1)S(1)} %pad_maximum_fusion.3.refs_10_), channel_id=1, source_target_pairs={{0,2},{2,4},{4,6},{6,8},{8,10},{10,12},{12,14},{14,0},{1,3},{3,5},... | collective-permute-start | bytes 1179656 | tf_op jit(solution)/shard_map/ppermute | solution.py:28
  25.7 9.5 %copy-start.16 = (bf16[2,16,6144]{2,1,0:T(8,128)(2,1)}, bf16[2,16,6144]{2,1,0:T(8,128)(2,1)S(1)}, u32[]{:S(2)}) copy-start(bf16[2,16,6144]{2,1,0:T(8,128)(2,1)S(1)} %collective-permute-done.4.refs_11_) | copy-start | bytes 1179652
  30.8 30.4 %copy-start.3 = (bf16[24,128,128]{2,1,0:T(8,128)(2,1)}, bf16[24,128,128]{2,1,0:T(8,128)(2,1)S(1)}, u32[]{:S(2)}) copy-start(bf16[24,128,128]{2,1,0:T(8,128)(2,1)S(1)} %collective-permute-done.1.refs_3_) | copy-start | bytes 2359300
  32.2 28.4 %collective-permute-start.7 = (bf16[48,128,128]{2,1,0:T(8,128)(2,1)}, bf16[48,128,128]{2,1,0:T(8,128)(2,1)}, u32[]{:S(2)}, u32[]{:S(2)}) collective-permute-start(bf16[48,128,128]{2,1,0:T(8,128)(2,1)} %pad_maximum_fusion), channel_id=1, source_target_pairs={{0,32},{1,97},{32,64},{33,1},{64,96},{65,33},{96,0},{97,65},{2,34}... | collective-permute-start | bytes 4718600 | tf_op jit(solution)/shard_map/ppermute | solution.py:43
  34.7 2.2 %collective-permute-start.12 = (bf16[2,16,6144]{2,1,0:T(8,128)(2,1)S(1)}, bf16[2,16,6144]{2,1,0:T(8,128)(2,1)S(1)}, u32[]{:S(2)}, u32[]{:S(2)}) collective-permute-start(bf16[2,16,6144]{2,1,0:T(8,128)(2,1)S(1)} %pad_maximum_fusion.3.refs_10_), channel_id=1, source_target_pairs={{0,1},{1,0},{2,3},{3,2},{4,5},{5,4},{6,7},{7,6},{8,9},{9,8},{10,11... | collective-permute-start | bytes 1179656 | tf_op jit(solution)/shard_map/ppermute | solution.py:33
  34.9 2.7 %collective-permute-start.13 = (bf16[2,16,6144]{2,1,0:T(8,128)(2,1)S(1)}, bf16[2,16,6144]{2,1,0:T(8,128)(2,1)S(1)}, u32[]{:S(2)}, u32[]{:S(2)}) collective-permute-start(bf16[2,16,6144]{2,1,0:T(8,128)(2,1)S(1)} %collective-permute-done.4.refs_11_), channel_id=1, source_target_pairs={{0,1},{1,0},{2,3},{3,2},{4,5},{5,4},{6,7},{7,6},{8,9},{9,8},{10,11... | collective-permute-start | bytes 1179656 | tf_op jit(solution)/shard_map/ppermute | solution.py:33
  35.2 10.6 %collective-permute-start.8 = (bf16[2,16,6144]{2,1,0:T(8,128)(2,1)S(1)}, bf16[2,16,6144]{2,1,0:T(8,128)(2,1)}, u32[]{:S(2)}, u32[]{:S(2)}) collective-permute-start(bf16[2,16,6144]{2,1,0:T(8,128)(2,1)S(1)} %collective-permute-done.4.refs_11_), channel_id=1, source_target_pairs={{0,2},{2,4},{4,6},{6,8},{8,10},{10,12},{12,14},{14,0},{1,3},{3,5},... | collective-permute-start | bytes 1179656 | tf_op jit(solution)/shard_map/ppermute | solution.py:28
  36.9 10.9 %collective-permute-start.10 = (bf16[2,16,6144]{2,1,0:T(8,128)(2,1)}, bf16[2,16,6144]{2,1,0:T(8,128)(2,1)}, u32[]{:S(2)}, u32[]{:S(2)}) collective-permute-start(bf16[2,16,6144]{2,1,0:T(8,128)(2,1)} %collective-permute-done.5.refs_14_), channel_id=1, source_target_pairs={{0,14},{2,0},{4,2},{6,4},{8,6},{10,8},{12,10},{14,12},{1,15},{3,1}... | collective-permute-start | bytes 1179656 | tf_op jit(solution)/shard_map/ppermute | solution.py:28
  36.9 10.6 %copy-start.17 = (bf16[2,16,6144]{2,1,0:T(8,128)(2,1)}, bf16[2,16,6144]{2,1,0:T(8,128)(2,1)S(1)}, u32[]{:S(2)}) copy-start(bf16[2,16,6144]{2,1,0:T(8,128)(2,1)S(1)} %collective-permute-done.12.refs_19_) | copy-start | bytes 1179652
  36.9 23.8 %collective-permute-start.6 = (bf16[24,128,128]{2,1,0:T(8,128)(2,1)S(1)}, bf16[24,128,128]{2,1,0:T(8,128)(2,1)S(1)}, u32[]{:S(2)}, u32[]{:S(2)}) collective-permute-start(bf16[24,128,128]{2,1,0:T(8,128)(2,1)S(1)} %collective-permute-done.refs_4_), channel_id=1, source_target_pairs={{0,128},{128,0},{1,129},{129,1},{2,130},{130,2},{3,131},{131,3},{4... | collective-permute-start | bytes 2359304 | tf_op jit(solution)/shard_map/ppermute | solution.py:33
  37.6 10.1 %copy-start.18 = (bf16[2,16,6144]{2,1,0:T(8,128)(2,1)}, bf16[2,16,6144]{2,1,0:T(8,128)(2,1)S(1)}, u32[]{:S(2)}) copy-start(bf16[2,16,6144]{2,1,0:T(8,128)(2,1)S(1)} %collective-permute-done.13.refs_20_) | copy-start | bytes 1179652
  37.6 13.5 %collective-permute-start.14 = (bf16[2,16,6144]{2,1,0:T(8,128)(2,1)}, bf16[2,16,6144]{2,1,0:T(8,128)(2,1)}, u32[]{:S(2)}, u32[]{:S(2)}) collective-permute-start(bf16[2,16,6144]{2,1,0:T(8,128)(2,1)} %collective-permute-done.5.refs_14_), channel_id=1, source_target_pairs={{0,1},{1,0},{2,3},{3,2},{4,5},{5,4},{6,7},{7,6},{8,9},{9,8},{10,11... | collective-permute-start | bytes 1179656 | tf_op jit(solution)/shard_map/ppermute | solution.py:33
  45.9 13.3 %collective-permute-start.9 = (bf16[2,16,6144]{2,1,0:T(8,128)(2,1)}, bf16[2,16,6144]{2,1,0:T(8,128)(2,1)S(1)}, u32[]{:S(2)}, u32[]{:S(2)}) collective-permute-start(bf16[2,16,6144]{2,1,0:T(8,128)(2,1)} %collective-permute-done.8.refs_12_), channel_id=1, source_target_pairs={{0,2},{2,4},{4,6},{6,8},{8,10},{10,12},{12,14},{14,0},{1,3},{3,5},... | collective-permute-start | bytes 1179656 | tf_op jit(solution)/shard_map/ppermute | solution.py:28
  47.8 12.9 %collective-permute-start.11 = (bf16[2,16,6144]{2,1,0:T(8,128)(2,1)}, bf16[2,16,6144]{2,1,0:T(8,128)(2,1)S(1)}, u32[]{:S(2)}, u32[]{:S(2)}) collective-permute-start(bf16[2,16,6144]{2,1,0:T(8,128)(2,1)} %collective-permute-done.10.refs_15_), channel_id=1, source_target_pairs={{0,14},{2,0},{4,2},{6,4},{8,6},{10,8},{12,10},{14,12},{1,15},{3,1}... | collective-permute-start | bytes 1179656 | tf_op jit(solution)/shard_map/ppermute | solution.py:28
  51.1 11.8 %collective-permute-start.18 = (bf16[2,16,6144]{2,1,0:T(8,128)(2,1)}, bf16[2,16,6144]{2,1,0:T(8,128)(2,1)S(1)}, u32[]{:S(2)}, u32[]{:S(2)}) collective-permute-start(bf16[2,16,6144]{2,1,0:T(8,128)(2,1)} %collective-permute-done.8.refs_12_), channel_id=1, source_target_pairs={{0,1},{1,0},{2,3},{3,2},{4,5},{5,4},{6,7},{7,6},{8,9},{9,8},{10,11... | collective-permute-start | bytes 1179656 | tf_op jit(solution)/shard_map/ppermute | solution.py:33
  59.2 6.1 %collective-permute-start.20 = (bf16[2,16,6144]{2,1,0:T(8,128)(2,1)}, bf16[2,16,6144]{2,1,0:T(8,128)(2,1)S(1)}, u32[]{:S(2)}, u32[]{:S(2)}) collective-permute-start(bf16[2,16,6144]{2,1,0:T(8,128)(2,1)} %collective-permute-done.10.refs_15_), channel_id=1, source_target_pairs={{0,1},{1,0},{2,3},{3,2},{4,5},{5,4},{6,7},{7,6},{8,9},{9,8},{10,11... | collective-permute-start | bytes 1179656 | tf_op jit(solution)/shard_map/ppermute | solution.py:33
  60.7 21.6 %copy-start.1 = (f32[12288]{0:T(1024)S(1)}, f32[12288]{0:T(1024)}, u32[]{:S(2)}) copy-start(f32[12288]{0:T(1024)} %param.10) | copy-start | bytes 147460
  60.7 12.9 %collective-permute-start.19 = (bf16[2,16,6144]{2,1,0:T(8,128)(2,1)S(1)}, bf16[2,16,6144]{2,1,0:T(8,128)(2,1)S(1)}, u32[]{:S(2)}, u32[]{:S(2)}) collective-permute-start(bf16[2,16,6144]{2,1,0:T(8,128)(2,1)S(1)} %collective-permute-done.9.refs_13_), channel_id=1, source_target_pairs={{0,1},{1,0},{2,3},{3,2},{4,5},{5,4},{6,7},{7,6},{8,9},{9,8},{10,11... | collective-permute-start | bytes 1179656 | tf_op jit(solution)/shard_map/ppermute | solution.py:33
  61.6 19.6 %collective-permute-start.15 = (bf16[48,128,128]{2,1,0:T(8,128)(2,1)S(1)}, bf16[48,128,128]{2,1,0:T(8,128)(2,1)S(1)}, u32[]{:S(2)}, u32[]{:S(2)}) collective-permute-start(bf16[48,128,128]{2,1,0:T(8,128)(2,1)S(1)} %pad_maximum_fusion.1), channel_id=1, source_target_pairs={{0,32},{1,97},{32,64},{33,1},{64,96},{65,33},{96,0},{97,65},{2,34}... | collective-permute-start | bytes 4718600 | tf_op jit(solution)/shard_map/ppermute | solution.py:43
  62.4 11.2 %collective-permute-start.21 = (bf16[2,16,6144]{2,1,0:T(8,128)(2,1)S(1)}, bf16[2,16,6144]{2,1,0:T(8,128)(2,1)S(1)}, u32[]{:S(2)}, u32[]{:S(2)}) collective-permute-start(bf16[2,16,6144]{2,1,0:T(8,128)(2,1)S(1)} %collective-permute-done.11.refs_16_), channel_id=1, source_target_pairs={{0,1},{1,0},{2,3},{3,2},{4,5},{5,4},{6,7},{7,6},{8,9},{9,8},{10,11... | collective-permute-start | bytes 1179656 | tf_op jit(solution)/shard_map/ppermute | solution.py:33
  62.9 18.2 %copy-start.19 = (bf16[2,16,6144]{2,1,0:T(8,128)(2,1)}, bf16[2,16,6144]{2,1,0:T(8,128)(2,1)S(1)}, u32[]{:S(2)}) copy-start(bf16[2,16,6144]{2,1,0:T(8,128)(2,1)S(1)} %collective-permute-done.18.refs_21_) | copy-start | bytes 1179652
  62.9 7.7 %collective-permute-start.17 = (bf16[16,6144]{1,0:T(8,128)(2,1)S(1)}, bf16[16,6144]{1,0:T(8,128)(2,1)S(1)}, u32[]{:S(2)}, u32[]{:S(2)}) collective-permute-start(bf16[16,6144]{1,0:T(8,128)(2,1)S(1)} %slice_bitcast_fusion.4), channel_id=1, source_target_pairs={{0,14},{2,0},{4,2},{6,4},{8,6},{10,8},{12,10},{14,12},{1,15},{3,1}... | collective-permute-start | bytes 589832 | tf_op jit(solution)/shard_map/ppermute | solution.py:28
  65.3 15.9 %copy-start.20 = (bf16[2,16,6144]{2,1,0:T(8,128)(2,1)}, bf16[2,16,6144]{2,1,0:T(8,128)(2,1)S(1)}, u32[]{:S(2)}) copy-start(bf16[2,16,6144]{2,1,0:T(8,128)(2,1)S(1)} %collective-permute-done.20.refs_24_) | copy-start | bytes 1179652
  65.3 7.4 %collective-permute-start.16 = (bf16[16,6144]{1,0:T(8,128)(2,1)S(1)}, bf16[16,6144]{1,0:T(8,128)(2,1)S(1)}, u32[]{:S(2)}, u32[]{:S(2)}) collective-permute-start(bf16[16,6144]{1,0:T(8,128)(2,1)S(1)} %slice_bitcast_fusion.5), channel_id=1, source_target_pairs={{0,2},{2,4},{4,6},{6,8},{8,10},{10,12},{12,14},{14,0},{1,3},{3,5},... | collective-permute-start | bytes 589832 | tf_op jit(solution)/shard_map/ppermute | solution.py:28
  70.6 3.0 %collective-permute-start.23 = (bf16[16,6144]{1,0:T(8,128)(2,1)S(1)}, bf16[16,6144]{1,0:T(8,128)(2,1)S(1)}, u32[]{:S(2)}, u32[]{:S(2)}) collective-permute-start(bf16[16,6144]{1,0:T(8,128)(2,1)S(1)} %collective-permute-done.17.refs_18_), channel_id=1, source_target_pairs={{0,1},{1,0},{2,3},{3,2},{4,5},{5,4},{6,7},{7,6},{8,9},{9,8},{10,11... | collective-permute-start | bytes 589832 | tf_op jit(solution)/shard_map/ppermute | solution.py:33
  72.7 1.9 collective-permute-start.22
  102.0 11.4 %copy-start.27 = (bf16[48,128,128]{2,1,0:T(8,128)(2,1)S(1)}, bf16[48,128,128]{2,1,0:T(8,128)(2,1)}, u32[]{:S(2)}) copy-start(bf16[48,128,128]{2,1,0:T(8,128)(2,1)} %get-tuple-element.89) | copy-start | bytes 4718596
  102.0 3.1 %collective-permute-start.24 = (f32[13824]{0:T(1024)S(1)}, f32[13824]{0:T(1024)S(1)}, u32[]{:S(2)}, u32[]{:S(2)}) collective-permute-start(f32[13824]{0:T(1024)S(1)} %pad_maximum_fusion.9), channel_id=1, source_target_pairs={{0,32},{32,0},{64,96},{96,64},{1,33},{33,1},{65,97},{97,65},{2,34}... | collective-permute-start | bytes 165896 | tf_op jit(solution)/shard_map/ppermute | solution.py:33
  102.6 7.1 %collective-permute-start.26 = (bf16[2,16,6144]{2,1,0:T(8,128)(2,1)}, bf16[2,16,6144]{2,1,0:T(8,128)(2,1)S(1)}, u32[]{:S(2)}, u32[]{:S(2)}) collective-permute-start(bf16[2,16,6144]{2,1,0:T(8,128)(2,1)} %get-tuple-element.75), channel_id=1, source_target_pairs={{0,1},{1,0},{2,3},{3,2},{4,5},{5,4},{6,7},{7,6},{8,9},{9,8},{10,11... | collective-permute-start | bytes 1179656 | tf_op jit(solution)/shard_map/ppermute | solution.py:33
  105.1 4.6 %collective-permute-start.25 = (f32[13824]{0:T(1024)S(1)}, f32[13824]{0:T(1024)S(1)}, u32[]{:S(2)}, u32[]{:S(2)}) collective-permute-start(f32[13824]{0:T(1024)S(1)} %fusion.36), channel_id=1, source_target_pairs={{0,64},{32,96},{64,0},{96,32},{1,65},{33,97},{65,1},{97,33},{2,66}... | collective-permute-start | bytes 165896 | tf_op jit(solution)/shard_map/ppermute | solution.py:33
  106.9 17.4 %collective-permute-start.30 = (bf16[7,2,16,6144]{3,2,1,0:T(8,128)(2,1)}, bf16[7,2,16,6144]{3,2,1,0:T(8,128)(2,1)S(1)}, u32[]{:S(2)}, u32[]{:S(2)}) collective-permute-start(bf16[7,2,16,6144]{3,2,1,0:T(8,128)(2,1)} %get-tuple-element.80), channel_id=1, source_target_pairs={{0,1},{1,0},{2,3},{3,2},{4,5},{5,4},{6,7},{7,6},{8,9},{9,8},{10,11... | collective-permute-start | bytes 8257544 | tf_op jit(solution)/shard_map/ppermute | solution.py:33
  109.9 14.4 %collective-permute-start.28 = (bf16[16,6144]{1,0:T(8,128)(2,1)S(1)}, bf16[16,6144]{1,0:T(8,128)(2,1)S(1)}, u32[]{:S(2)}, u32[]{:S(2)}) collective-permute-start(bf16[16,6144]{1,0:T(8,128)(2,1)S(1)} %get-tuple-element.136), channel_id=1, source_target_pairs={{0,14},{2,0},{4,2},{6,4},{8,6},{10,8},{12,10},{14,12},{1,15},{3,1}... | collective-permute-start | bytes 589832 | tf_op jit(solution)/shard_map/ppermute | solution.py:28
  112.7 11.7 %collective-permute-start.27 = (bf16[16,6144]{1,0:T(8,128)(2,1)S(1)}, bf16[16,6144]{1,0:T(8,128)(2,1)S(1)}, u32[]{:S(2)}, u32[]{:S(2)}) collective-permute-start(bf16[16,6144]{1,0:T(8,128)(2,1)S(1)} %get-tuple-element.137), channel_id=1, source_target_pairs={{0,2},{2,4},{4,6},{6,8},{8,10},{10,12},{12,14},{14,0},{1,3},{3,5},... | collective-permute-start | bytes 589832 | tf_op jit(solution)/shard_map/ppermute | solution.py:28
  112.7 11.7 %collective-permute-start.29 = (f32[13824]{0:T(1024)S(1)}, f32[13824]{0:T(1024)S(1)}, u32[]{:S(2)}, u32[]{:S(2)}) collective-permute-start(f32[13824]{0:T(1024)S(1)} %add.189), channel_id=1, source_target_pairs={{0,128},{128,0},{1,129},{129,1},{2,130},{130,2},{3,131},{131,3},{4... | collective-permute-start | bytes 165896 | tf_op jit(solution)/shard_map/ppermute | solution.py:33
  113.4 30.3 %collective-permute-start.34 = (bf16[48,128,128]{2,1,0:T(8,128)(2,1)S(1)}, bf16[48,128,128]{2,1,0:T(8,128)(2,1)S(1)}, u32[]{:S(2)}, u32[]{:S(2)}) collective-permute-start(bf16[48,128,128]{2,1,0:T(8,128)(2,1)S(1)} %copy-done.27), channel_id=1, source_target_pairs={{0,96},{1,33},{32,0},{33,65},{64,32},{65,97},{96,64},{97,1},{2,98}... | collective-permute-start | bytes 4718600 | tf_op jit(solution)/shard_map/ppermute | solution.py:43
  124.6 19.1 %copy-start.13 = (bf16[24,128,128]{2,1,0:T(8,128)(2,1)S(1)}, bf16[24,128,128]{2,1,0:T(8,128)(2,1)}, u32[]{:S(2)}) copy-start(bf16[24,128,128]{2,1,0:T(8,128)(2,1)} %get-tuple-element.97) | copy-start | bytes 2359300
  124.6 19.1 %copy-start.14 = (bf16[24,128,128]{2,1,0:T(8,128)(2,1)S(1)}, bf16[24,128,128]{2,1,0:T(8,128)(2,1)}, u32[]{:S(2)}) copy-start(bf16[24,128,128]{2,1,0:T(8,128)(2,1)} %get-tuple-element.95) | copy-start | bytes 2359300
  124.7 18.9 %collective-permute-start.31 = (bf16[2,16,6144]{2,1,0:T(8,128)(2,1)S(1)}, bf16[2,16,6144]{2,1,0:T(8,128)(2,1)S(1)}, u32[]{:S(2)}, u32[]{:S(2)}) collective-permute-start(bf16[2,16,6144]{2,1,0:T(8,128)(2,1)S(1)} %pad_maximum_fusion.4), channel_id=1, source_target_pairs={{0,2},{2,4},{4,6},{6,8},{8,10},{10,12},{12,14},{14,0},{1,3},{3,5},... | collective-permute-start | bytes 1179656 | tf_op jit(solution)/shard_map/ppermute | solution.py:28
  127.5 16.2 %collective-permute-start.32 = (bf16[2,16,6144]{2,1,0:T(8,128)(2,1)S(1)}, bf16[2,16,6144]{2,1,0:T(8,128)(2,1)S(1)}, u32[]{:S(2)}, u32[]{:S(2)}) collective-permute-start(bf16[2,16,6144]{2,1,0:T(8,128)(2,1)S(1)} %pad_maximum_fusion.5), channel_id=1, source_target_pairs={{0,14},{2,0},{4,2},{6,4},{8,6},{10,8},{12,10},{14,12},{1,15},{3,1}... | collective-permute-start | bytes 1179656 | tf_op jit(solution)/shard_map/ppermute | solution.py:28
  127.7 16.0 %collective-permute-start.33 = (f32[12288]{0:T(1024)S(1)}, f32[12288]{0:T(1024)S(1)}, u32[]{:S(2)}, u32[]{:S(2)}) collective-permute-start(f32[12288]{0:T(1024)S(1)} %slice.139), channel_id=1, source_target_pairs={{0,16},{16,0},{1,17},{17,1},{2,18},{18,2},{3,19},{19,3},{4,20},{20... | collective-permute-start | bytes 147464 | tf_op jit(solution)/shard_map/ppermute | solution.py:33
  129.1 31.6 %collective-permute-start.38 = (bf16[48,128,128]{2,1,0:T(8,128)(2,1)S(1)}, bf16[48,128,128]{2,1,0:T(8,128)(2,1)S(1)}, u32[]{:S(2)}, u32[]{:S(2)}) collective-permute-start(bf16[48,128,128]{2,1,0:T(8,128)(2,1)S(1)} %copy-done.26), channel_id=1, source_target_pairs={{0,96},{1,33},{32,0},{33,65},{64,32},{65,97},{96,64},{97,1},{2,98}... | collective-permute-start | bytes 4718600 | tf_op jit(solution)/shard_map/ppermute | solution.py:43
  144.3 16.4 %collective-permute-start.39 = (bf16[24,128,128]{2,1,0:T(8,128)(2,1)S(1)}, bf16[24,128,128]{2,1,0:T(8,128)(2,1)S(1)}, u32[]{:S(2)}, u32[]{:S(2)}) collective-permute-start(bf16[24,128,128]{2,1,0:T(8,128)(2,1)S(1)} %get-tuple-element.131), channel_id=1, source_target_pairs={{0,128},{128,0},{1,129},{129,1},{2,130},{130,2},{3,131},{131,3},{4... | collective-permute-start | bytes 2359304 | tf_op jit(solution)/shard_map/ppermute | solution.py:33
  147.0 13.6 %collective-permute-start.36 = (bf16[2,16,6144]{2,1,0:T(8,128)(2,1)S(1)}, bf16[2,16,6144]{2,1,0:T(8,128)(2,1)S(1)}, u32[]{:S(2)}, u32[]{:S(2)}) collective-permute-start(bf16[2,16,6144]{2,1,0:T(8,128)(2,1)S(1)} %get-tuple-element.124), channel_id=1, source_target_pairs={{0,14},{2,0},{4,2},{6,4},{8,6},{10,8},{12,10},{14,12},{1,15},{3,1}... | collective-permute-start | bytes 1179656 | tf_op jit(solution)/shard_map/ppermute | solution.py:28
  149.1 11.6 %collective-permute-start.35 = (bf16[2,16,6144]{2,1,0:T(8,128)(2,1)S(1)}, bf16[2,16,6144]{2,1,0:T(8,128)(2,1)S(1)}, u32[]{:S(2)}, u32[]{:S(2)}) collective-permute-start(bf16[2,16,6144]{2,1,0:T(8,128)(2,1)S(1)} %get-tuple-element.125), channel_id=1, source_target_pairs={{0,2},{2,4},{4,6},{6,8},{8,10},{10,12},{12,14},{14,0},{1,3},{3,5},... | collective-permute-start | bytes 1179656 | tf_op jit(solution)/shard_map/ppermute | solution.py:28
  149.7 11.0 %collective-permute-start.37 = (f32[12288]{0:T(1024)S(1)}, f32[12288]{0:T(1024)S(1)}, u32[]{:S(2)}, u32[]{:S(2)}) collective-permute-start(f32[12288]{0:T(1024)S(1)} %slice_add_fusion.1), channel_id=1, source_target_pairs={{0,2},{2,0},{4,6},{6,4},{8,10},{10,8},{12,14},{14,12},{1,3},{3,1},... | collective-permute-start | bytes 147464 | tf_op jit(solution)/shard_map/ppermute | solution.py:33
  160.7 8.1 %copy-start.15 = (bf16[24,128,128]{2,1,0:T(8,128)(2,1)S(1)}, bf16[24,128,128]{2,1,0:T(8,128)(2,1)}, u32[]{:S(2)}) copy-start(bf16[24,128,128]{2,1,0:T(8,128)(2,1)} %get-tuple-element.105) | copy-start | bytes 2359300
  161.0 11.8 %collective-permute-start.41 = (bf16[2,16,6144]{2,1,0:T(8,128)(2,1)S(1)}, bf16[2,16,6144]{2,1,0:T(8,128)(2,1)S(1)}, u32[]{:S(2)}, u32[]{:S(2)}) collective-permute-start(bf16[2,16,6144]{2,1,0:T(8,128)(2,1)S(1)} %get-tuple-element.122), channel_id=1, source_target_pairs={{0,14},{2,0},{4,2},{6,4},{8,6},{10,8},{12,10},{14,12},{1,15},{3,1}... | collective-permute-start | bytes 1179656 | tf_op jit(solution)/shard_map/ppermute | solution.py:28
  163.3 9.5 %collective-permute-start.40 = (bf16[2,16,6144]{2,1,0:T(8,128)(2,1)S(1)}, bf16[2,16,6144]{2,1,0:T(8,128)(2,1)S(1)}, u32[]{:S(2)}, u32[]{:S(2)}) collective-permute-start(bf16[2,16,6144]{2,1,0:T(8,128)(2,1)S(1)} %get-tuple-element.123), channel_id=1, source_target_pairs={{0,2},{2,4},{4,6},{6,8},{8,10},{10,12},{12,14},{14,0},{1,3},{3,5},... | collective-permute-start | bytes 1179656 | tf_op jit(solution)/shard_map/ppermute | solution.py:28
  163.7 9.0 %collective-permute-start.42 = (f32[12288]{0:T(1024)S(1)}, f32[12288]{0:T(1024)S(1)}, u32[]{:S(2)}, u32[]{:S(2)}) collective-permute-start(f32[12288]{0:T(1024)S(1)} %add.207), channel_id=1, source_target_pairs={{0,4},{2,6},{4,0},{6,2},{8,12},{10,14},{12,8},{14,10},{1,5},{3,7},... | collective-permute-start | bytes 147464 | tf_op jit(solution)/shard_map/ppermute | solution.py:33
  169.2 20.6 %collective-permute-start.45 = (bf16[24,128,128]{2,1,0:T(8,128)(2,1)S(1)}, bf16[24,128,128]{2,1,0:T(8,128)(2,1)S(1)}, u32[]{:S(2)}, u32[]{:S(2)}) collective-permute-start(bf16[24,128,128]{2,1,0:T(8,128)(2,1)S(1)} %add_convert_fusion), channel_id=1, source_target_pairs={{0,64},{32,96},{64,0},{96,32},{1,65},{33,97},{65,1},{97,33},{2,66}... | collective-permute-start | bytes 2359304 | tf_op jit(solution)/shard_map/ppermute | solution.py:33
  170.4 19.4 %collective-permute-start.46 = (bf16[24,128,128]{2,1,0:T(8,128)(2,1)S(1)}, bf16[24,128,128]{2,1,0:T(8,128)(2,1)S(1)}, u32[]{:S(2)}, u32[]{:S(2)}) collective-permute-start(bf16[24,128,128]{2,1,0:T(8,128)(2,1)S(1)} %get-tuple-element.108), channel_id=1, source_target_pairs={{0,128},{128,0},{1,129},{129,1},{2,130},{130,2},{3,131},{131,3},{4... | collective-permute-start | bytes 2359304 | tf_op jit(solution)/shard_map/ppermute | solution.py:33
  172.9 24.5 %copy-start.12 = (bf16[24,128,128]{2,1,0:T(8,128)(2,1)S(1)}, bf16[24,128,128]{2,1,0:T(8,128)(2,1)}, u32[]{:S(2)}) copy-start(bf16[24,128,128]{2,1,0:T(8,128)(2,1)} %get-tuple-element.111) | copy-start | bytes 2359300
  173.0 16.8 %collective-permute-start.43 = (bf16[2,8,6144]{2,1,0:T(8,128)(2,1)S(1)}, bf16[2,8,6144]{2,1,0:T(8,128)(2,1)S(1)}, u32[]{:S(2)}, u32[]{:S(2)}) collective-permute-start(bf16[2,8,6144]{2,1,0:T(8,128)(2,1)S(1)} %slice.229), channel_id=1, source_target_pairs={{0,16},{16,0},{1,17},{17,1},{2,18},{18,2},{3,19},{19,3},{4,20},{20... | collective-permute-start | bytes 589832 | tf_op jit(solution)/shard_map/ppermute | solution.py:33
  174.7 6.8 %collective-permute-start.44 = (f32[12288]{0:T(1024)S(1)}, f32[12288]{0:T(1024)S(1)}, u32[]{:S(2)}, u32[]{:S(2)}) collective-permute-start(f32[12288]{0:T(1024)S(1)} %add.210), channel_id=1, source_target_pairs={{0,8},{2,10},{4,12},{6,14},{8,0},{10,2},{12,4},{14,6},{1,9},{3,11}... | collective-permute-start | bytes 147464 | tf_op jit(solution)/shard_map/ppermute | solution.py:33
  189.8 9.5 %collective-permute-start.48 = (f32[12288]{0:T(1024)S(1)}, f32[12288]{0:T(1024)S(1)}, u32[]{:S(2)}, u32[]{:S(2)}) collective-permute-start(f32[12288]{0:T(1024)S(1)} %add.216), channel_id=1, source_target_pairs={{0,1},{1,0},{2,3},{3,2},{4,5},{5,4},{6,7},{7,6},{8,9},{9,8},{10,11... | collective-permute-start | bytes 147464 | tf_op jit(solution)/shard_map/ppermute | solution.py:33
  197.3 2.7 %collective-permute-start.47 = (bf16[2,4,6144]{2,1,0:T(4,128)(2,1)S(1)}, bf16[2,4,6144]{2,1,0:T(4,128)(2,1)S(1)}, u32[]{:S(2)}, u32[]{:S(2)}) collective-permute-start(bf16[2,4,6144]{2,1,0:T(4,128)(2,1)S(1)} %select_convert_fusion), channel_id=1, source_target_pairs={{0,1},{1,0},{2,3},{3,2},{4,5},{5,4},{6,7},{7,6},{8,9},{9,8},{10,11... | collective-permute-start | bytes 294920 | tf_op jit(solution)/shard_map/ppermute | solution.py:33
  (13 other events, 49.9 us)
where the time goes:
time: 205 us; the launch traced here: 201 us
  starting transfers between devices  83.2 us (41%)
  waiting for transfers between devices  81.1 us (40%)
  Pallas kernels  19.6 us (10%)
  other arithmetic  13 us (6%)
  local copies, waits for them, and re-layouts  3.1 us (2%)
    ppermute x29, starting transfers between devices, swap(): return lax.ppermute(value, axis, [(i, i ^ bit) for i in range(count)])  46.9 us
    ppermute x16, waiting for transfers between devices, shift(): lax.ppermute(value, axis, [(i, (i + steps) % count) for i in range(count)])  32 us
    ppermute x4, waiting for transfers between devices, step_x(): return lax.ppermute(value, ('x', 'c'), pairs)  29 us
    ppermute x16, starting transfers between devices, shift(): lax.ppermute(value, axis, [(i, (i + steps) % count) for i in range(count)])  21.2 us
    ppermute x29, waiting for transfers between devices, swap(): return lax.ppermute(value, axis, [(i, i ^ bit) for i in range(count)])  20.1 us
    pallas_call x1, Pallas kernels, compute(): pl.pallas_call(compute_kernel, out_shape=out_shape, in_specs=[smem, smem]...  19.6 us
    ppermute x4, starting transfers between devices, step_x(): return lax.ppermute(value, ('x', 'c'), pairs)  15.1 us
  transfers between devices with their start and end apart: 49, of which 18 were waited for; matrix products, arithmetic and copies ran while one was open for 4% of the time, Pallas kernels for 0%

commit v1 on v0

--- a/solution.py
+++ b/solution.py
@@ -53,10 +53,10 @@
     bias, gain = refs[8:10]
     near, far = refs[10:19], refs[19:28]
     keep = refs[28:36]
-    send_last, send_rest = refs[36:38]
-    grads = refs[38:44]
-    bias_sum, gain_sum = refs[44:46]
-    x_all, dy_all, out_acc, in_acc, sems = refs[46:]
+    send = refs[36]
+    grads = refs[37:43]
+    bias_sum, gain_sum = refs[43:45]
+    x_all, dy_all, out_acc, in_acc, sems = refs[45:]
 
     mine = pl.multiple_of(core[0] * HALF, BS)
     other = pl.multiple_of((1 - core[0]) * HALF, BS)
@@ -120,8 +120,7 @@
         rows = pl.ds(j * STRIP, STRIP)
         for part, acc in ((0, out_acc), (1, in_acc)):
             keep[j][part] = acc[rows, pl.ds(mine, HALF)].astype(BF16)
-            target = send_last.at[part] if j == 7 else send_rest.at[j, part]
-            target[...] = acc[rows, pl.ds(other, HALF)].astype(BF16)
+            send[j, part] = acc[rows, pl.ds(other, HALF)].astype(BF16)
 
     def gain_strip(b, carry):
         span = pl.ds(pl.multiple_of(b * 4 * BS, BS), 4 * BS)
@@ -138,8 +137,8 @@
     anyspace = pl.BlockSpec(memory_space=pl.ANY)
     part = jax.ShapeDtypeStruct((2, STRIP, HALF), BF16)
     out_shape = (
-        [part] * 9
-        + [jax.ShapeDtypeStruct((7, 2, STRIP, HALF), BF16)]
+        [part] * 8
+        + [jax.ShapeDtypeStruct((8, 2, STRIP, HALF), BF16)]
         + [jax.ShapeDtypeStruct(t.shape, BF16) for t in tiles]
         + [jax.ShapeDtypeStruct((HID, 1, BS), F32), jax.ShapeDtypeStruct((1, D), F32)]
     )
@@ -161,7 +160,7 @@
         ),
         name="butterfly_ffn",
     )(cols, core, *tiles, bias, gain, *near, *far)
-    return outs[:8], outs[8], outs[9], outs[10:16], outs[16], outs[17]
+    return outs[:8], outs[8], outs[9:15], outs[15], outs[16]
 
 
 def add(a, b):
@@ -225,7 +224,7 @@
     near = [piece, r1, r2, r3, l1, l2, l3, x4, dy4]
     far = [c_piece, c_r1, c_r2, c_r3, c_l1, c_l2, c_l3, c_x4, c_dy4]
 
-    keep, send_last, send_rest, grads, bias_part, gain_part = compute(
+    keep, send, grads, bias_part, gain_part = compute(
         cols,
         core.reshape(1),
         [near_t, far_t, near2_t, far2_t, near_odd, far_odd],
@@ -238,17 +237,16 @@
     sums = jnp.concatenate([gain_part[0], bias_part.reshape(HID * BS)])
     p0, m1, m2, m3, q1, q2, q3, p4 = keep
 
-    last = swap(send_last, "c", 1)
-    rest = swap(send_rest, "c", 1)
+    rest = swap(send, "c", 1)
     sums = sums + swap(sums, "x", 1)
     came_s = swap(sums, "x", 2)
-    came_s, last, g_fo, g_no = together(came_s, last, g_fo, g_no)
+    came_s, rest, g_fo, g_no = together(came_s, rest, g_fo, g_no)
     from_fo, from_no = step_x(g_fo, -1), step_x(g_no, -1)
     sums = sums + came_s
-    p4 = add(p4, last)
+    p4 = add(p4, rest[7])
     up_half, down_half = shift(p4[0], "z", 1), shift(p4[1], "z", -1)
     came_s = swap(sums, "yh", 1)
-    up_half, down_half, came_s, rest = together(up_half, down_half, came_s, rest)
+    up_half, down_half, came_s = together(up_half, down_half, came_s)
     sums = sums + came_s
     grad_bias, grad_gain = sums[D:], sums[:D]
     q3, m3 = add3(q3, rest[6]), add3(m3, rest[3])

time: 205 us -> 212 us (1.034)
  waiting for transfers between devices: 81.1 us -> 91 us
  starting transfers between devices: 83.2 us -> 75 us
  other arithmetic: 13 us -> 17.8 us
    ppermute x29 -> x28, waiting for transfers between devices: 20.1 us -> 31.4 us  [swap(): return lax.ppermute(value, axis, [(i, i ^ bit) for i in range(count)])]
    ppermute x29 -> x28, starting transfers between devices: 46.9 us -> 39.8 us  [swap(): return lax.ppermute(value, axis, [(i, i ^ bit) for i in range(count)])]
    ppermute x4, waiting for transfers between devices: 29 us -> 22.3 us  [step_x(): return lax.ppermute(value, ('x', 'c'), pairs)]
    ppermute x16, waiting for transfers between devices: 32 us -> 37.3 us  [shift(): lax.ppermute(value, axis, [(i, (i + steps) % count) for i in range(count)])]
    add x3, other arithmetic: 0.83 us -> 3.21 us  [add3(): return sum((v.astype(F32) for v in values))]
  transfers between devices with their start and end apart: 49 -> 48, of which waited for: 18 -> 23; matrix products, arithmetic and copies ran while one was open for 4% -> 4% of each run, Pallas kernels for 0% -> 0%
where the time goes in v1:
time: 212 us; the launch traced here: 208 us
  waiting for transfers between devices  91 us (43%)
  starting transfers between devices  75 us (35%)
  Pallas kernels  19.6 us (9%)
  other arithmetic  17.8 us (8%)
  local copies, waits for them, and re-layouts  3.1 us (1%)
    ppermute x28, starting transfers between devices, swap(): return lax.ppermute(value, axis, [(i, i ^ bit) for i in range(count)])  39.8 us
    ppermute x16, waiting for transfers between devices, shift(): lax.ppermute(value, axis, [(i, (i + steps) % count) for i in range(count)])  37.3 us
    ppermute x28, waiting for transfers between devices, swap(): return lax.ppermute(value, axis, [(i, i ^ bit) for i in range(count)])  31.4 us
    ppermute x4, waiting for transfers between devices, step_x(): return lax.ppermute(value, ('x', 'c'), pairs)  22.3 us
    ppermute x16, starting transfers between devices, shift(): lax.ppermute(value, axis, [(i, (i + steps) % count) for i in range(count)])  21.6 us
    pallas_call x1, Pallas kernels, compute(): pl.pallas_call(compute_kernel, out_shape=out_shape, in_specs=[smem, smem]...  19.6 us
    ppermute x4, starting transfers between devices, step_x(): return lax.ppermute(value, ('x', 'c'), pairs)  13.6 us
  transfers between devices with their start and end apart: 48, of which 23 were waited for; matrix products, arithmetic and copies ran while one was open for 4% of the time, Pallas kernels for 0%

profile of v1, /device:TPU:41, one launch (start us, length us, event | category | flops | bytes accessed | tf_op | source)
XLA Modules:
  0.0 207.8 jit_solution(13656612546996850770)
XLA Ops:
  0.7 1.2 fusion.26
  1.9 1.0 fusion.35
  2.9 0.9 broadcast_select_fusion.2
  3.8 0.8 collective-permute-start.2
  5.5 1.0 broadcast_select_fusion.1
  7.1 2.4 %collective-permute-start.1 = (bf16[24,128,128]{2,1,0:T(8,128)(2,1)S(1)}, bf16[24,128,128]{2,1,0:T(8,128)(2,1)S(1)}, u32[]{:S(2)}, u32[]{:S(2)}) collective-permute-start(bf16[24,128,128]{2,1,0:T(8,128)(2,1)S(1)} %pad_maximum_fusion.2.refs_2_), channel_id=1, source_target_pairs={{0,128},{128,0},{1,129},{129,1},{2,130},{130,2},{3,131},{131,3},{4... | collective-permute-start | bytes 2359304 | tf_op jit(solution)/shard_map/ppermute | solution.py:33
  9.5 2.7 %collective-permute-start = (bf16[24,128,128]{2,1,0:T(8,128)(2,1)S(1)}, bf16[24,128,128]{2,1,0:T(8,128)(2,1)S(1)}, u32[]{:S(2)}, u32[]{:S(2)}) collective-permute-start(bf16[24,128,128]{2,1,0:T(8,128)(2,1)S(1)} %pad_maximum_fusion.2.refs_2_), channel_id=1, source_target_pairs={{0,64},{32,96},{64,0},{96,32},{1,65},{33,97},{65,1},{97,33},{2,66}... | collective-permute-start | bytes 2359304 | tf_op jit(solution)/shard_map/ppermute | solution.py:33
  13.7 1.1 collective-permute-start.4
  14.8 7.4 %collective-permute-done.5.refs_14_ = bf16[2,16,6144]{2,1,0:T(8,128)(2,1)} collective-permute-done((bf16[2,16,6144]{2,1,0:T(8,128)(2,1)S(1)}, bf16[2,16,6144]{2,1,0:T(8,128)(2,1)}, u32[]{:S(2)}, u32[]{:S(2)}) %collective-permute-start.5) | collective-permute-done | bytes 393248 | tf_op jit(solution)/shard_map/ppermute | solution.py:28
  22.2 3.5 %collective-permute-done.4.refs_11_ = bf16[2,16,6144]{2,1,0:T(8,128)(2,1)S(1)} collective-permute-done((bf16[2,16,6144]{2,1,0:T(8,128)(2,1)S(1)}, bf16[2,16,6144]{2,1,0:T(8,128)(2,1)S(1)}, u32[]{:S(2)}, u32[]{:S(2)}) %collective-permute-start.4) | collective-permute-done | bytes 393248 | tf_op jit(solution)/shard_map/ppermute | solution.py:28
  25.7 5.0 %collective-permute-done.1.refs_3_ = bf16[24,128,128]{2,1,0:T(8,128)(2,1)S(1)} collective-permute-done((bf16[24,128,128]{2,1,0:T(8,128)(2,1)S(1)}, bf16[24,128,128]{2,1,0:T(8,128)(2,1)S(1)}, u32[]{:S(2)}, u32[]{:S(2)}) %collective-permute-start.1) | collective-permute-done | bytes 786464 | tf_op jit(solution)/shard_map/ppermute | solution.py:33
  30.7 1.5 pad_maximum_fusion
  32.2 2.5 %collective-permute-start.7 = (bf16[48,128,128]{2,1,0:T(8,128)(2,1)}, bf16[48,128,128]{2,1,0:T(8,128)(2,1)}, u32[]{:S(2)}, u32[]{:S(2)}) collective-permute-start(bf16[48,128,128]{2,1,0:T(8,128)(2,1)} %pad_maximum_fusion), channel_id=1, source_target_pairs={{0,32},{1,97},{32,64},{33,1},{64,96},{65,33},{96,0},{97,65},{2,34}... | collective-permute-start | bytes 4718600 | tf_op jit(solution)/shard_map/ppermute | solution.py:43
  35.2 1.6 collective-permute-start.8
  36.8 0.7 collective-permute-start.6
  37.6 0.8 collective-permute-start.14
  38.4 7.4 %collective-permute-done.8.refs_12_ = bf16[2,16,6144]{2,1,0:T(8,128)(2,1)} collective-permute-done((bf16[2,16,6144]{2,1,0:T(8,128)(2,1)S(1)}, bf16[2,16,6144]{2,1,0:T(8,128)(2,1)}, u32[]{:S(2)}, u32[]{:S(2)}) %collective-permute-start.8) | collective-permute-done | bytes 393248 | tf_op jit(solution)/shard_map/ppermute | solution.py:28
  45.8 1.6 collective-permute-start.9
  47.7 2.5 %collective-permute-start.11 = (bf16[2,16,6144]{2,1,0:T(8,128)(2,1)}, bf16[2,16,6144]{2,1,0:T(8,128)(2,1)S(1)}, u32[]{:S(2)}, u32[]{:S(2)}) collective-permute-start(bf16[2,16,6144]{2,1,0:T(8,128)(2,1)} %collective-permute-done.10.refs_15_), channel_id=1, source_target_pairs={{0,14},{2,0},{4,2},{6,4},{8,6},{10,8},{12,10},{14,12},{1,15},{3,1}... | collective-permute-start | bytes 1179656 | tf_op jit(solution)/shard_map/ppermute | solution.py:28
  51.0 1.1 collective-permute-start.18
  52.1 7.0 %collective-permute-done.9.refs_13_ = bf16[2,16,6144]{2,1,0:T(8,128)(2,1)S(1)} collective-permute-done((bf16[2,16,6144]{2,1,0:T(8,128)(2,1)}, bf16[2,16,6144]{2,1,0:T(8,128)(2,1)S(1)}, u32[]{:S(2)}, u32[]{:S(2)}) %collective-permute-start.9) | collective-permute-done | bytes 393248 | tf_op jit(solution)/shard_map/ppermute | solution.py:28
  59.1 1.5 collective-permute-start.20
  61.5 0.8 collective-permute-start.15
  62.8 2.4 %collective-permute-start.17 = (bf16[16,6144]{1,0:T(8,128)(2,1)S(1)}, bf16[16,6144]{1,0:T(8,128)(2,1)S(1)}, u32[]{:S(2)}, u32[]{:S(2)}) collective-permute-start(bf16[16,6144]{1,0:T(8,128)(2,1)S(1)} %slice_bitcast_fusion.4), channel_id=1, source_target_pairs={{0,14},{2,0},{4,2},{6,4},{8,6},{10,8},{12,10},{14,12},{1,15},{3,1}... | collective-permute-start | bytes 589832 | tf_op jit(solution)/shard_map/ppermute | solution.py:28
  65.5 5.0 %collective-permute-done.17.refs_18_ = bf16[16,6144]{1,0:T(8,128)(2,1)S(1)} collective-permute-done((bf16[16,6144]{1,0:T(8,128)(2,1)S(1)}, bf16[16,6144]{1,0:T(8,128)(2,1)S(1)}, u32[]{:S(2)}, u32[]{:S(2)}) %collective-permute-start.17) | collective-permute-done | bytes 196640 | tf_op jit(solution)/shard_map/ppermute | solution.py:28
  71.2 1.4 collective-permute-done.16.refs_17_
  72.7 0.9 collective-permute-start.22
  73.6 1.0 collective-permute-done.22.refs_26_
  74.6 6.5 %collective-permute-done.15.refs_7_ = bf16[48,128,128]{2,1,0:T(8,128)(2,1)S(1)} collective-permute-done((bf16[48,128,128]{2,1,0:T(8,128)(2,1)S(1)}, bf16[48,128,128]{2,1,0:T(8,128)(2,1)S(1)}, u32[]{:S(2)}, u32[]{:S(2)}) %collective-permute-start.15) | collective-permute-done | bytes 1572896 | tf_op jit(solution)/shard_map/ppermute | solution.py:43
  81.1 1.1 copy-done.8
  82.3 19.6 %butterfly_ffn.1 = (bf16[2,16,6144]{2,1,0:T(8,128)(2,1)S(1)}, bf16[2,16,6144]{2,1,0:T(8,128)(2,1)S(1)}, bf16[2,16,6144]{2,1,0:T(8,128)(2,1)S(1)}, bf16[2,16,6144...) custom-call(s32[12,8]{1,0:T(8,128)S(1)} %select_bitcast_fusion.refs_, ...), custom_call_target="tpu_custom_call" | custom-call | flops 2400000000 | bytes 25000000 | tf_op jit(solution)/shard_map/butterfly_ffn/pallas_call | solution.py:145
  101.9 2.4 %collective-permute-start.26 = (bf16[8,2,16,6144]{3,2,1,0:T(8,128)(2,1)}, bf16[8,2,16,6144]{3,2,1,0:T(8,128)(2,1)}, u32[]{:S(2)}, u32[]{:S(2)}) collective-permute-start(bf16[8,2,16,6144]{3,2,1,0:T(8,128)(2,1)} %get-tuple-element.72), channel_id=1, source_target_pairs={{0,1},{1,0},{2,3},{3,2},{4,5},{5,4},{6,7},{7,6},{8,9},{9,8},{10,11... | collective-permute-start | bytes 9437192 | tf_op jit(solution)/shard_map/ppermute | solution.py:33
  104.5 3.5 %collective-permute-done.24 = f32[13824]{0:T(1024)S(1)} collective-permute-done((f32[13824]{0:T(1024)S(1)}, f32[13824]{0:T(1024)S(1)}, u32[]{:S(2)}, u32[]{:S(2)}) %collective-permute-start.24) | collective-permute-done | bytes 55328 | tf_op jit(solution)/shard_map/ppermute | solution.py:33
  108.7 4.0 %collective-permute-done.25 = f32[13824]{0:T(1024)S(1)} collective-permute-done((f32[13824]{0:T(1024)S(1)}, f32[13824]{0:T(1024)S(1)}, u32[]{:S(2)}, u32[]{:S(2)}) %collective-permute-start.25) | collective-permute-done | bytes 55328 | tf_op jit(solution)/shard_map/ppermute | solution.py:33
  112.6 1.5 convert_add_fusion.3
  114.2 2.4 %collective-permute-start.28 = (bf16[16,6144]{1,0:T(8,128)(2,1)S(1)}, bf16[16,6144]{1,0:T(8,128)(2,1)S(1)}, u32[]{:S(2)}, u32[]{:S(2)}) collective-permute-start(bf16[16,6144]{1,0:T(8,128)(2,1)S(1)} %get-tuple-element.133), channel_id=1, source_target_pairs={{0,14},{2,0},{4,2},{6,4},{8,6},{10,8},{12,10},{14,12},{1,15},{3,1}... | collective-permute-start | bytes 589832 | tf_op jit(solution)/shard_map/ppermute | solution.py:28
  116.9 0.7 collective-permute-start.29
  117.7 10.2 %collective-permute-start.33 = (bf16[48,128,128]{2,1,0:T(8,128)(2,1)S(1)}, bf16[48,128,128]{2,1,0:T(8,128)(2,1)S(1)}, u32[]{:S(2)}, u32[]{:S(2)}) collective-permute-start(bf16[48,128,128]{2,1,0:T(8,128)(2,1)S(1)} %copy-done.27), channel_id=1, source_target_pairs={{0,96},{1,33},{32,0},{33,65},{64,32},{65,97},{96,64},{97,1},{2,98}... | collective-permute-start | bytes 4718600 | tf_op jit(solution)/shard_map/ppermute | solution.py:43
  128.1 2.3 %collective-permute-start.31 = (bf16[2,16,6144]{2,1,0:T(8,128)(2,1)S(1)}, bf16[2,16,6144]{2,1,0:T(8,128)(2,1)S(1)}, u32[]{:S(2)}, u32[]{:S(2)}) collective-permute-start(bf16[2,16,6144]{2,1,0:T(8,128)(2,1)S(1)} %pad_maximum_fusion.5), channel_id=1, source_target_pairs={{0,14},{2,0},{4,2},{6,4},{8,6},{10,8},{12,10},{14,12},{1,15},{3,1}... | collective-permute-start | bytes 1179656 | tf_op jit(solution)/shard_map/ppermute | solution.py:28
  131.1 1.4 collective-permute-start.32
  132.5 1.9 collective-permute-done.32
  134.4 3.6 %collective-permute-done.31 = bf16[2,16,6144]{2,1,0:T(8,128)(2,1)S(1)} collective-permute-done((bf16[2,16,6144]{2,1,0:T(8,128)(2,1)S(1)}, bf16[2,16,6144]{2,1,0:T(8,128)(2,1)S(1)}, u32[]{:S(2)}, u32[]{:S(2)}) %collective-permute-start.31) | collective-permute-done | bytes 393248 | tf_op jit(solution)/shard_map/ppermute | solution.py:28
  138.0 1.7 collective-permute-done.30
  139.7 8.5 %collective-permute-done.33 = bf16[48,128,128]{2,1,0:T(8,128)(2,1)S(1)} collective-permute-done((bf16[48,128,128]{2,1,0:T(8,128)(2,1)S(1)}, bf16[48,128,128]{2,1,0:T(8,128)(2,1)S(1)}, u32[]{:S(2)}, u32[]{:S(2)}) %collective-permute-start.33) | collective-permute-done | bytes 1572896 | tf_op jit(solution)/shard_map/ppermute | solution.py:43
  148.3 0.8 add_convert_fusion.1
  149.0 2.4 %collective-permute-start.38 = (bf16[24,128,128]{2,1,0:T(8,128)(2,1)S(1)}, bf16[24,128,128]{2,1,0:T(8,128)(2,1)S(1)}, u32[]{:S(2)}, u32[]{:S(2)}) collective-permute-start(bf16[24,128,128]{2,1,0:T(8,128)(2,1)S(1)} %get-tuple-element.128), channel_id=1, source_target_pairs={{0,128},{128,0},{1,129},{129,1},{2,130},{130,2},{3,131},{131,3},{4... | collective-permute-start | bytes 2359304 | tf_op jit(solution)/shard_map/ppermute | solution.py:33
  151.5 1.4 fusion.5
  152.9 2.3 %collective-permute-start.35 = (bf16[2,16,6144]{2,1,0:T(8,128)(2,1)S(1)}, bf16[2,16,6144]{2,1,0:T(8,128)(2,1)S(1)}, u32[]{:S(2)}, u32[]{:S(2)}) collective-permute-start(bf16[2,16,6144]{2,1,0:T(8,128)(2,1)S(1)} %get-tuple-element.120), channel_id=1, source_target_pairs={{0,14},{2,0},{4,2},{6,4},{8,6},{10,8},{12,10},{14,12},{1,15},{3,1}... | collective-permute-start | bytes 1179656 | tf_op jit(solution)/shard_map/ppermute | solution.py:28
  155.8 2.1 %collective-permute-start.36 = (f32[12288]{0:T(1024)S(1)}, f32[12288]{0:T(1024)S(1)}, u32[]{:S(2)}, u32[]{:S(2)}) collective-permute-start(f32[12288]{0:T(1024)S(1)} %slice_add_fusion.1), channel_id=1, source_target_pairs={{0,2},{2,0},{4,6},{6,4},{8,10},{10,8},{12,14},{14,12},{1,3},{3,1},... | collective-permute-start | bytes 147464 | tf_op jit(solution)/shard_map/ppermute | solution.py:33
  157.9 7.4 %collective-permute-done.37 = bf16[48,128,128]{2,1,0:T(8,128)(2,1)S(1)} collective-permute-done((bf16[48,128,128]{2,1,0:T(8,128)(2,1)S(1)}, bf16[48,128,128]{2,1,0:T(8,128)(2,1)S(1)}, u32[]{:S(2)}, u32[]{:S(2)}) %collective-permute-start.37) | collective-permute-done | bytes 1572896 | tf_op jit(solution)/shard_map/ppermute | solution.py:43
  165.3 1.9 collective-permute-done.38
  167.2 1.5 fusion.3
  168.7 2.3 %collective-permute-start.40 = (bf16[2,16,6144]{2,1,0:T(8,128)(2,1)S(1)}, bf16[2,16,6144]{2,1,0:T(8,128)(2,1)S(1)}, u32[]{:S(2)}, u32[]{:S(2)}) collective-permute-start(bf16[2,16,6144]{2,1,0:T(8,128)(2,1)S(1)} %get-tuple-element.118), channel_id=1, source_target_pairs={{0,14},{2,0},{4,2},{6,4},{8,6},{10,8},{12,10},{14,12},{1,15},{3,1}... | collective-permute-start | bytes 1179656 | tf_op jit(solution)/shard_map/ppermute | solution.py:28
  171.6 4.6 %collective-permute-start.41 = (f32[12288]{0:T(1024)S(1)}, f32[12288]{0:T(1024)S(1)}, u32[]{:S(2)}, u32[]{:S(2)}) collective-permute-start(f32[12288]{0:T(1024)S(1)} %add.207), channel_id=1, source_target_pairs={{0,4},{2,6},{4,0},{6,2},{8,12},{10,14},{12,8},{14,10},{1,5},{3,7},... | collective-permute-start | bytes 147464 | tf_op jit(solution)/shard_map/ppermute | solution.py:33
  176.8 2.4 %collective-permute-start.45 = (bf16[24,128,128]{2,1,0:T(8,128)(2,1)S(1)}, bf16[24,128,128]{2,1,0:T(8,128)(2,1)S(1)}, u32[]{:S(2)}, u32[]{:S(2)}) collective-permute-start(bf16[24,128,128]{2,1,0:T(8,128)(2,1)S(1)} %get-tuple-element.104), channel_id=1, source_target_pairs={{0,128},{128,0},{1,129},{129,1},{2,130},{130,2},{3,131},{131,3},{4... | collective-permute-start | bytes 2359304 | tf_op jit(solution)/shard_map/ppermute | solution.py:33
  179.2 0.8 collective-permute-done.41
  180.0 1.2 fusion.12
  181.3 1.4 collective-permute-start.42
  182.7 2.5 %collective-permute-start.43 = (f32[12288]{0:T(1024)S(1)}, f32[12288]{0:T(1024)S(1)}, u32[]{:S(2)}, u32[]{:S(2)}) collective-permute-start(f32[12288]{0:T(1024)S(1)} %add.210), channel_id=1, source_target_pairs={{0,8},{2,10},{4,12},{6,14},{8,0},{10,2},{12,4},{14,6},{1,9},{3,11}... | collective-permute-start | bytes 147464 | tf_op jit(solution)/shard_map/ppermute | solution.py:33
  185.8 3.7 %collective-permute-done.43 = f32[12288]{0:T(1024)S(1)} collective-permute-done((f32[12288]{0:T(1024)S(1)}, f32[12288]{0:T(1024)S(1)}, u32[]{:S(2)}, u32[]{:S(2)}) %collective-permute-start.43) | collective-permute-done | bytes 49184 | tf_op jit(solution)/shard_map/ppermute | solution.py:33
  189.5 8.5 %collective-permute-done.42 = bf16[2,8,6144]{2,1,0:T(8,128)(2,1)S(1)} collective-permute-done((bf16[2,8,6144]{2,1,0:T(8,128)(2,1)S(1)}, bf16[2,8,6144]{2,1,0:T(8,128)(2,1)S(1)}, u32[]{:S(2)}, u32[]{:S(2)}) %collective-permute-start.42) | collective-permute-done | bytes 196640 | tf_op jit(solution)/shard_map/ppermute | solution.py:33
  198.1 5.5 %collective-permute-start.47 = (f32[12288]{0:T(1024)S(1)}, f32[12288]{0:T(1024)S(1)}, u32[]{:S(2)}, u32[]{:S(2)}) collective-permute-start(f32[12288]{0:T(1024)S(1)} %add.216), channel_id=1, source_target_pairs={{0,1},{1,0},{2,3},{3,2},{4,5},{5,4},{6,7},{7,6},{8,9},{9,8},{10,11... | collective-permute-start | bytes 147464 | tf_op jit(solution)/shard_map/ppermute | solution.py:33
  204.4 1.4 fusion
  206.8 0.9 fusion.25
  (146 shorter events, 13.3 us)
Async XLA Ops:
  0.6 49.7 %copy-start = (s32[12,8]{0,1:T(8,128)S(1)}, s32[12,8]{0,1:T(8,128)}, u32[]{:S(2)}) copy-start(s32[12,8]{0,1:T(8,128)} %param.14) | copy-start | bytes 1156
  3.8 1.7 collective-permute-start.2
  6.6 6.2 %collective-permute-start.3 = (bf16[2,8,6144]{2,1,0:T(8,128)(2,1)S(1)}, bf16[2,8,6144]{2,1,0:T(8,128)(2,1)S(1)}, u32[]{:S(2)}, u32[]{:S(2)}) collective-permute-start(bf16[2,8,6144]{2,1,0:T(8,128)(2,1)S(1)} %pad_maximum_fusion.7), channel_id=1, source_target_pairs={{0,16},{16,0},{1,17},{17,1},{2,18},{18,2},{3,19},{19,3},{4,20},{20... | collective-permute-start | bytes 589832 | tf_op jit(solution)/shard_map/ppermute | solution.py:33
  7.1 23.6 %collective-permute-start.1 = (bf16[24,128,128]{2,1,0:T(8,128)(2,1)S(1)}, bf16[24,128,128]{2,1,0:T(8,128)(2,1)S(1)}, u32[]{:S(2)}, u32[]{:S(2)}) collective-permute-start(bf16[24,128,128]{2,1,0:T(8,128)(2,1)S(1)} %pad_maximum_fusion.2.refs_2_), channel_id=1, source_target_pairs={{0,128},{128,0},{1,129},{129,1},{2,130},{130,2},{3,131},{131,3},{4... | collective-permute-start | bytes 2359304 | tf_op jit(solution)/shard_map/ppermute | solution.py:33
  9.5 21.2 %collective-permute-start = (bf16[24,128,128]{2,1,0:T(8,128)(2,1)S(1)}, bf16[24,128,128]{2,1,0:T(8,128)(2,1)S(1)}, u32[]{:S(2)}, u32[]{:S(2)}) collective-permute-start(bf16[24,128,128]{2,1,0:T(8,128)(2,1)S(1)} %pad_maximum_fusion.2.refs_2_), channel_id=1, source_target_pairs={{0,64},{32,96},{64,0},{96,32},{1,65},{33,97},{65,1},{97,33},{2,66}... | collective-permute-start | bytes 2359304 | tf_op jit(solution)/shard_map/ppermute | solution.py:33
  13.0 21.7 %copy-start.6 = (bf16[2,16,6144]{2,1,0:T(8,128)(2,1)}, bf16[2,16,6144]{2,1,0:T(8,128)(2,1)S(1)}, u32[]{:S(2)}) copy-start(bf16[2,16,6144]{2,1,0:T(8,128)(2,1)S(1)} %pad_maximum_fusion.3.refs_10_) | copy-start | bytes 1179652
  13.0 37.9 %copy-start.25 = (f32[1536]{0:T(1024)S(1)}, f32[1536]{0:T(1024)}, u32[]{:S(2)}) copy-start(f32[1536]{0:T(1024)} %param.11) | copy-start | bytes 18436
  13.0 9.2 %collective-permute-start.5 = (bf16[2,16,6144]{2,1,0:T(8,128)(2,1)S(1)}, bf16[2,16,6144]{2,1,0:T(8,128)(2,1)}, u32[]{:S(2)}, u32[]{:S(2)}) collective-permute-start(bf16[2,16,6144]{2,1,0:T(8,128)(2,1)S(1)} %pad_maximum_fusion.3.refs_10_), channel_id=1, source_target_pairs={{0,14},{2,0},{4,2},{6,4},{8,6},{10,8},{12,10},{14,12},{1,15},{3,1}... | collective-permute-start | bytes 1179656 | tf_op jit(solution)/shard_map/ppermute | solution.py:28
  13.7 12.0 %collective-permute-start.4 = (bf16[2,16,6144]{2,1,0:T(8,128)(2,1)S(1)}, bf16[2,16,6144]{2,1,0:T(8,128)(2,1)S(1)}, u32[]{:S(2)}, u32[]{:S(2)}) collective-permute-start(bf16[2,16,6144]{2,1,0:T(8,128)(2,1)S(1)} %pad_maximum_fusion.3.refs_10_), channel_id=1, source_target_pairs={{0,2},{2,4},{4,6},{6,8},{8,10},{10,12},{12,14},{14,0},{1,3},{3,5},... | collective-permute-start | bytes 1179656 | tf_op jit(solution)/shard_map/ppermute | solution.py:28
  25.7 9.5 %copy-start.16 = (bf16[2,16,6144]{2,1,0:T(8,128)(2,1)}, bf16[2,16,6144]{2,1,0:T(8,128)(2,1)S(1)}, u32[]{:S(2)}) copy-start(bf16[2,16,6144]{2,1,0:T(8,128)(2,1)S(1)} %collective-permute-done.4.refs_11_) | copy-start | bytes 1179652
  30.7 30.4 %copy-start.3 = (bf16[24,128,128]{2,1,0:T(8,128)(2,1)}, bf16[24,128,128]{2,1,0:T(8,128)(2,1)S(1)}, u32[]{:S(2)}) copy-start(bf16[24,128,128]{2,1,0:T(8,128)(2,1)S(1)} %collective-permute-done.1.refs_3_) | copy-start | bytes 2359300
  32.2 28.4 %collective-permute-start.7 = (bf16[48,128,128]{2,1,0:T(8,128)(2,1)}, bf16[48,128,128]{2,1,0:T(8,128)(2,1)}, u32[]{:S(2)}, u32[]{:S(2)}) collective-permute-start(bf16[48,128,128]{2,1,0:T(8,128)(2,1)} %pad_maximum_fusion), channel_id=1, source_target_pairs={{0,32},{1,97},{32,64},{33,1},{64,96},{65,33},{96,0},{97,65},{2,34}... | collective-permute-start | bytes 4718600 | tf_op jit(solution)/shard_map/ppermute | solution.py:43
  34.7 2.2 %collective-permute-start.12 = (bf16[2,16,6144]{2,1,0:T(8,128)(2,1)S(1)}, bf16[2,16,6144]{2,1,0:T(8,128)(2,1)S(1)}, u32[]{:S(2)}, u32[]{:S(2)}) collective-permute-start(bf16[2,16,6144]{2,1,0:T(8,128)(2,1)S(1)} %pad_maximum_fusion.3.refs_10_), channel_id=1, source_target_pairs={{0,1},{1,0},{2,3},{3,2},{4,5},{5,4},{6,7},{7,6},{8,9},{9,8},{10,11... | collective-permute-start | bytes 1179656 | tf_op jit(solution)/shard_map/ppermute | solution.py:33
  34.9 2.7 %collective-permute-start.13 = (bf16[2,16,6144]{2,1,0:T(8,128)(2,1)S(1)}, bf16[2,16,6144]{2,1,0:T(8,128)(2,1)S(1)}, u32[]{:S(2)}, u32[]{:S(2)}) collective-permute-start(bf16[2,16,6144]{2,1,0:T(8,128)(2,1)S(1)} %collective-permute-done.4.refs_11_), channel_id=1, source_target_pairs={{0,1},{1,0},{2,3},{3,2},{4,5},{5,4},{6,7},{7,6},{8,9},{9,8},{10,11... | collective-permute-start | bytes 1179656 | tf_op jit(solution)/shard_map/ppermute | solution.py:33
  35.2 10.6 %collective-permute-start.8 = (bf16[2,16,6144]{2,1,0:T(8,128)(2,1)S(1)}, bf16[2,16,6144]{2,1,0:T(8,128)(2,1)}, u32[]{:S(2)}, u32[]{:S(2)}) collective-permute-start(bf16[2,16,6144]{2,1,0:T(8,128)(2,1)S(1)} %collective-permute-done.4.refs_11_), channel_id=1, source_target_pairs={{0,2},{2,4},{4,6},{6,8},{8,10},{10,12},{12,14},{14,0},{1,3},{3,5},... | collective-permute-start | bytes 1179656 | tf_op jit(solution)/shard_map/ppermute | solution.py:28
  36.8 10.9 %collective-permute-start.10 = (bf16[2,16,6144]{2,1,0:T(8,128)(2,1)}, bf16[2,16,6144]{2,1,0:T(8,128)(2,1)}, u32[]{:S(2)}, u32[]{:S(2)}) collective-permute-start(bf16[2,16,6144]{2,1,0:T(8,128)(2,1)} %collective-permute-done.5.refs_14_), channel_id=1, source_target_pairs={{0,14},{2,0},{4,2},{6,4},{8,6},{10,8},{12,10},{14,12},{1,15},{3,1}... | collective-permute-start | bytes 1179656 | tf_op jit(solution)/shard_map/ppermute | solution.py:28
  36.8 10.6 %copy-start.17 = (bf16[2,16,6144]{2,1,0:T(8,128)(2,1)}, bf16[2,16,6144]{2,1,0:T(8,128)(2,1)S(1)}, u32[]{:S(2)}) copy-start(bf16[2,16,6144]{2,1,0:T(8,128)(2,1)S(1)} %collective-permute-done.12.refs_19_) | copy-start | bytes 1179652
  36.8 23.8 %collective-permute-start.6 = (bf16[24,128,128]{2,1,0:T(8,128)(2,1)S(1)}, bf16[24,128,128]{2,1,0:T(8,128)(2,1)S(1)}, u32[]{:S(2)}, u32[]{:S(2)}) collective-permute-start(bf16[24,128,128]{2,1,0:T(8,128)(2,1)S(1)} %collective-permute-done.refs_4_), channel_id=1, source_target_pairs={{0,128},{128,0},{1,129},{129,1},{2,130},{130,2},{3,131},{131,3},{4... | collective-permute-start | bytes 2359304 | tf_op jit(solution)/shard_map/ppermute | solution.py:33
  37.6 10.1 %copy-start.18 = (bf16[2,16,6144]{2,1,0:T(8,128)(2,1)}, bf16[2,16,6144]{2,1,0:T(8,128)(2,1)S(1)}, u32[]{:S(2)}) copy-start(bf16[2,16,6144]{2,1,0:T(8,128)(2,1)S(1)} %collective-permute-done.13.refs_20_) | copy-start | bytes 1179652
  37.6 13.5 %collective-permute-start.14 = (bf16[2,16,6144]{2,1,0:T(8,128)(2,1)}, bf16[2,16,6144]{2,1,0:T(8,128)(2,1)}, u32[]{:S(2)}, u32[]{:S(2)}) collective-permute-start(bf16[2,16,6144]{2,1,0:T(8,128)(2,1)} %collective-permute-done.5.refs_14_), channel_id=1, source_target_pairs={{0,1},{1,0},{2,3},{3,2},{4,5},{5,4},{6,7},{7,6},{8,9},{9,8},{10,11... | collective-permute-start | bytes 1179656 | tf_op jit(solution)/shard_map/ppermute | solution.py:33
  45.8 13.3 %collective-permute-start.9 = (bf16[2,16,6144]{2,1,0:T(8,128)(2,1)}, bf16[2,16,6144]{2,1,0:T(8,128)(2,1)S(1)}, u32[]{:S(2)}, u32[]{:S(2)}) collective-permute-start(bf16[2,16,6144]{2,1,0:T(8,128)(2,1)} %collective-permute-done.8.refs_12_), channel_id=1, source_target_pairs={{0,2},{2,4},{4,6},{6,8},{8,10},{10,12},{12,14},{14,0},{1,3},{3,5},... | collective-permute-start | bytes 1179656 | tf_op jit(solution)/shard_map/ppermute | solution.py:28
  47.7 12.9 %collective-permute-start.11 = (bf16[2,16,6144]{2,1,0:T(8,128)(2,1)}, bf16[2,16,6144]{2,1,0:T(8,128)(2,1)S(1)}, u32[]{:S(2)}, u32[]{:S(2)}) collective-permute-start(bf16[2,16,6144]{2,1,0:T(8,128)(2,1)} %collective-permute-done.10.refs_15_), channel_id=1, source_target_pairs={{0,14},{2,0},{4,2},{6,4},{8,6},{10,8},{12,10},{14,12},{1,15},{3,1}... | collective-permute-start | bytes 1179656 | tf_op jit(solution)/shard_map/ppermute | solution.py:28
  51.0 11.8 %collective-permute-start.18 = (bf16[2,16,6144]{2,1,0:T(8,128)(2,1)}, bf16[2,16,6144]{2,1,0:T(8,128)(2,1)S(1)}, u32[]{:S(2)}, u32[]{:S(2)}) collective-permute-start(bf16[2,16,6144]{2,1,0:T(8,128)(2,1)} %collective-permute-done.8.refs_12_), channel_id=1, source_target_pairs={{0,1},{1,0},{2,3},{3,2},{4,5},{5,4},{6,7},{7,6},{8,9},{9,8},{10,11... | collective-permute-start | bytes 1179656 | tf_op jit(solution)/shard_map/ppermute | solution.py:33
  59.1 6.1 %collective-permute-start.20 = (bf16[2,16,6144]{2,1,0:T(8,128)(2,1)}, bf16[2,16,6144]{2,1,0:T(8,128)(2,1)S(1)}, u32[]{:S(2)}, u32[]{:S(2)}) collective-permute-start(bf16[2,16,6144]{2,1,0:T(8,128)(2,1)} %collective-permute-done.10.refs_15_), channel_id=1, source_target_pairs={{0,1},{1,0},{2,3},{3,2},{4,5},{5,4},{6,7},{7,6},{8,9},{9,8},{10,11... | collective-permute-start | bytes 1179656 | tf_op jit(solution)/shard_map/ppermute | solution.py:33
  60.6 21.6 %copy-start.1 = (f32[12288]{0:T(1024)S(1)}, f32[12288]{0:T(1024)}, u32[]{:S(2)}) copy-start(f32[12288]{0:T(1024)} %param.10) | copy-start | bytes 147460
  60.7 12.9 %collective-permute-start.19 = (bf16[2,16,6144]{2,1,0:T(8,128)(2,1)S(1)}, bf16[2,16,6144]{2,1,0:T(8,128)(2,1)S(1)}, u32[]{:S(2)}, u32[]{:S(2)}) collective-permute-start(bf16[2,16,6144]{2,1,0:T(8,128)(2,1)S(1)} %collective-permute-done.9.refs_13_), channel_id=1, source_target_pairs={{0,1},{1,0},{2,3},{3,2},{4,5},{5,4},{6,7},{7,6},{8,9},{9,8},{10,11... | collective-permute-start | bytes 1179656 | tf_op jit(solution)/shard_map/ppermute | solution.py:33
  61.5 19.6 %collective-permute-start.15 = (bf16[48,128,128]{2,1,0:T(8,128)(2,1)S(1)}, bf16[48,128,128]{2,1,0:T(8,128)(2,1)S(1)}, u32[]{:S(2)}, u32[]{:S(2)}) collective-permute-start(bf16[48,128,128]{2,1,0:T(8,128)(2,1)S(1)} %pad_maximum_fusion.1), channel_id=1, source_target_pairs={{0,32},{1,97},{32,64},{33,1},{64,96},{65,33},{96,0},{97,65},{2,34}... | collective-permute-start | bytes 4718600 | tf_op jit(solution)/shard_map/ppermute | solution.py:43
  62.4 11.2 %collective-permute-start.21 = (bf16[2,16,6144]{2,1,0:T(8,128)(2,1)S(1)}, bf16[2,16,6144]{2,1,0:T(8,128)(2,1)S(1)}, u32[]{:S(2)}, u32[]{:S(2)}) collective-permute-start(bf16[2,16,6144]{2,1,0:T(8,128)(2,1)S(1)} %collective-permute-done.11.refs_16_), channel_id=1, source_target_pairs={{0,1},{1,0},{2,3},{3,2},{4,5},{5,4},{6,7},{7,6},{8,9},{9,8},{10,11... | collective-permute-start | bytes 1179656 | tf_op jit(solution)/shard_map/ppermute | solution.py:33
  62.8 18.2 %copy-start.19 = (bf16[2,16,6144]{2,1,0:T(8,128)(2,1)}, bf16[2,16,6144]{2,1,0:T(8,128)(2,1)S(1)}, u32[]{:S(2)}) copy-start(bf16[2,16,6144]{2,1,0:T(8,128)(2,1)S(1)} %collective-permute-done.18.refs_21_) | copy-start | bytes 1179652
  62.8 7.7 %collective-permute-start.17 = (bf16[16,6144]{1,0:T(8,128)(2,1)S(1)}, bf16[16,6144]{1,0:T(8,128)(2,1)S(1)}, u32[]{:S(2)}, u32[]{:S(2)}) collective-permute-start(bf16[16,6144]{1,0:T(8,128)(2,1)S(1)} %slice_bitcast_fusion.4), channel_id=1, source_target_pairs={{0,14},{2,0},{4,2},{6,4},{8,6},{10,8},{12,10},{14,12},{1,15},{3,1}... | collective-permute-start | bytes 589832 | tf_op jit(solution)/shard_map/ppermute | solution.py:28
  65.2 15.9 %copy-start.20 = (bf16[2,16,6144]{2,1,0:T(8,128)(2,1)}, bf16[2,16,6144]{2,1,0:T(8,128)(2,1)S(1)}, u32[]{:S(2)}) copy-start(bf16[2,16,6144]{2,1,0:T(8,128)(2,1)S(1)} %collective-permute-done.20.refs_24_) | copy-start | bytes 1179652
  65.2 7.4 %collective-permute-start.16 = (bf16[16,6144]{1,0:T(8,128)(2,1)S(1)}, bf16[16,6144]{1,0:T(8,128)(2,1)S(1)}, u32[]{:S(2)}, u32[]{:S(2)}) collective-permute-start(bf16[16,6144]{1,0:T(8,128)(2,1)S(1)} %slice_bitcast_fusion.5), channel_id=1, source_target_pairs={{0,2},{2,4},{4,6},{6,8},{8,10},{10,12},{12,14},{14,0},{1,3},{3,5},... | collective-permute-start | bytes 589832 | tf_op jit(solution)/shard_map/ppermute | solution.py:28
  70.6 3.0 %collective-permute-start.23 = (bf16[16,6144]{1,0:T(8,128)(2,1)S(1)}, bf16[16,6144]{1,0:T(8,128)(2,1)S(1)}, u32[]{:S(2)}, u32[]{:S(2)}) collective-permute-start(bf16[16,6144]{1,0:T(8,128)(2,1)S(1)} %collective-permute-done.17.refs_18_), channel_id=1, source_target_pairs={{0,1},{1,0},{2,3},{3,2},{4,5},{5,4},{6,7},{7,6},{8,9},{9,8},{10,11... | collective-permute-start | bytes 589832 | tf_op jit(solution)/shard_map/ppermute | solution.py:33
  72.7 1.9 collective-permute-start.22
  73.6 7.5 %copy-start.21 = (bf16[2,16,6144]{2,1,0:T(8,128)(2,1)}, bf16[2,16,6144]{2,1,0:T(8,128)(2,1)S(1)}, u32[]{:S(2)}) copy-start(bf16[2,16,6144]{2,1,0:T(8,128)(2,1)S(1)} %collective-permute-done.19.refs_22_) | copy-start | bytes 1179652
  101.9 10.7 %collective-permute-start.26 = (bf16[8,2,16,6144]{3,2,1,0:T(8,128)(2,1)}, bf16[8,2,16,6144]{3,2,1,0:T(8,128)(2,1)}, u32[]{:S(2)}, u32[]{:S(2)}) collective-permute-start(bf16[8,2,16,6144]{3,2,1,0:T(8,128)(2,1)} %get-tuple-element.72), channel_id=1, source_target_pairs={{0,1},{1,0},{2,3},{3,2},{4,5},{5,4},{6,7},{7,6},{8,9},{9,8},{10,11... | collective-permute-start | bytes 9437192 | tf_op jit(solution)/shard_map/ppermute | solution.py:33
  104.4 3.6 %collective-permute-start.24 = (f32[13824]{0:T(1024)S(1)}, f32[13824]{0:T(1024)S(1)}, u32[]{:S(2)}, u32[]{:S(2)}) collective-permute-start(f32[13824]{0:T(1024)S(1)} %pad_maximum_fusion.9), channel_id=1, source_target_pairs={{0,32},{32,0},{64,96},{96,64},{1,33},{33,1},{65,97},{97,65},{2,34}... | collective-permute-start | bytes 165896 | tf_op jit(solution)/shard_map/ppermute | solution.py:33
  108.0 4.6 %collective-permute-start.25 = (f32[13824]{0:T(1024)S(1)}, f32[13824]{0:T(1024)S(1)}, u32[]{:S(2)}, u32[]{:S(2)}) collective-permute-start(f32[13824]{0:T(1024)S(1)} %fusion.37), channel_id=1, source_target_pairs={{0,64},{32,96},{64,0},{96,32},{1,65},{33,97},{65,1},{97,33},{2,66}... | collective-permute-start | bytes 165896 | tf_op jit(solution)/shard_map/ppermute | solution.py:33
  114.2 13.8 %collective-permute-start.28 = (bf16[16,6144]{1,0:T(8,128)(2,1)S(1)}, bf16[16,6144]{1,0:T(8,128)(2,1)S(1)}, u32[]{:S(2)}, u32[]{:S(2)}) collective-permute-start(bf16[16,6144]{1,0:T(8,128)(2,1)S(1)} %get-tuple-element.133), channel_id=1, source_target_pairs={{0,14},{2,0},{4,2},{6,4},{8,6},{10,8},{12,10},{14,12},{1,15},{3,1}... | collective-permute-start | bytes 589832 | tf_op jit(solution)/shard_map/ppermute | solution.py:28
  116.6 11.4 %collective-permute-start.27 = (bf16[16,6144]{1,0:T(8,128)(2,1)S(1)}, bf16[16,6144]{1,0:T(8,128)(2,1)S(1)}, u32[]{:S(2)}, u32[]{:S(2)}) collective-permute-start(bf16[16,6144]{1,0:T(8,128)(2,1)S(1)} %get-tuple-element.134), channel_id=1, source_target_pairs={{0,2},{2,4},{4,6},{6,8},{8,10},{10,12},{12,14},{14,0},{1,3},{3,5},... | collective-permute-start | bytes 589832 | tf_op jit(solution)/shard_map/ppermute | solution.py:28
  116.9 11.1 %collective-permute-start.29 = (f32[13824]{0:T(1024)S(1)}, f32[13824]{0:T(1024)S(1)}, u32[]{:S(2)}, u32[]{:S(2)}) collective-permute-start(f32[13824]{0:T(1024)S(1)} %add.193), channel_id=1, source_target_pairs={{0,128},{128,0},{1,129},{129,1},{2,130},{130,2},{3,131},{131,3},{4... | collective-permute-start | bytes 165896 | tf_op jit(solution)/shard_map/ppermute | solution.py:33
  117.7 14.8 %copy-start.26 = (bf16[48,128,128]{2,1,0:T(8,128)(2,1)S(1)}, bf16[48,128,128]{2,1,0:T(8,128)(2,1)}, u32[]{:S(2)}) copy-start(bf16[48,128,128]{2,1,0:T(8,128)(2,1)} %get-tuple-element.90) | copy-start | bytes 4718596
  117.7 30.5 %copy-start.13 = (bf16[24,128,128]{2,1,0:T(8,128)(2,1)S(1)}, bf16[24,128,128]{2,1,0:T(8,128)(2,1)}, u32[]{:S(2)}) copy-start(bf16[24,128,128]{2,1,0:T(8,128)(2,1)} %get-tuple-element.93) | copy-start | bytes 2359300
  117.7 30.5 %copy-start.14 = (bf16[24,128,128]{2,1,0:T(8,128)(2,1)S(1)}, bf16[24,128,128]{2,1,0:T(8,128)(2,1)}, u32[]{:S(2)}) copy-start(bf16[24,128,128]{2,1,0:T(8,128)(2,1)} %get-tuple-element.91) | copy-start | bytes 2359300
  117.7 30.5 %collective-permute-start.33 = (bf16[48,128,128]{2,1,0:T(8,128)(2,1)S(1)}, bf16[48,128,128]{2,1,0:T(8,128)(2,1)S(1)}, u32[]{:S(2)}, u32[]{:S(2)}) collective-permute-start(bf16[48,128,128]{2,1,0:T(8,128)(2,1)S(1)} %copy-done.27), channel_id=1, source_target_pairs={{0,96},{1,33},{32,0},{33,65},{64,32},{65,97},{96,64},{97,1},{2,98}... | collective-permute-start | bytes 4718600 | tf_op jit(solution)/shard_map/ppermute | solution.py:43
  128.1 9.9 %collective-permute-start.31 = (bf16[2,16,6144]{2,1,0:T(8,128)(2,1)S(1)}, bf16[2,16,6144]{2,1,0:T(8,128)(2,1)S(1)}, u32[]{:S(2)}, u32[]{:S(2)}) collective-permute-start(bf16[2,16,6144]{2,1,0:T(8,128)(2,1)S(1)} %pad_maximum_fusion.5), channel_id=1, source_target_pairs={{0,14},{2,0},{4,2},{6,4},{8,6},{10,8},{12,10},{14,12},{1,15},{3,1}... | collective-permute-start | bytes 1179656 | tf_op jit(solution)/shard_map/ppermute | solution.py:28
  130.5 9.3 %collective-permute-start.30 = (bf16[2,16,6144]{2,1,0:T(8,128)(2,1)S(1)}, bf16[2,16,6144]{2,1,0:T(8,128)(2,1)S(1)}, u32[]{:S(2)}, u32[]{:S(2)}) collective-permute-start(bf16[2,16,6144]{2,1,0:T(8,128)(2,1)S(1)} %pad_maximum_fusion.4), channel_id=1, source_target_pairs={{0,2},{2,4},{4,6},{6,8},{8,10},{10,12},{12,14},{14,0},{1,3},{3,5},... | collective-permute-start | bytes 1179656 | tf_op jit(solution)/shard_map/ppermute | solution.py:28
  131.1 3.3 %collective-permute-start.32 = (f32[12288]{0:T(1024)S(1)}, f32[12288]{0:T(1024)S(1)}, u32[]{:S(2)}, u32[]{:S(2)}) collective-permute-start(f32[12288]{0:T(1024)S(1)} %slice.143), channel_id=1, source_target_pairs={{0,16},{16,0},{1,17},{17,1},{2,18},{18,2},{3,19},{19,3},{4,20},{20... | collective-permute-start | bytes 147464 | tf_op jit(solution)/shard_map/ppermute | solution.py:33
  132.5 32.8 %collective-permute-start.37 = (bf16[48,128,128]{2,1,0:T(8,128)(2,1)S(1)}, bf16[48,128,128]{2,1,0:T(8,128)(2,1)S(1)}, u32[]{:S(2)}, u32[]{:S(2)}) collective-permute-start(bf16[48,128,128]{2,1,0:T(8,128)(2,1)S(1)} %copy-done.26), channel_id=1, source_target_pairs={{0,96},{1,33},{32,0},{33,65},{64,32},{65,97},{96,64},{97,1},{2,98}... | collective-permute-start | bytes 4718600 | tf_op jit(solution)/shard_map/ppermute | solution.py:43
  149.0 18.2 %collective-permute-start.38 = (bf16[24,128,128]{2,1,0:T(8,128)(2,1)S(1)}, bf16[24,128,128]{2,1,0:T(8,128)(2,1)S(1)}, u32[]{:S(2)}, u32[]{:S(2)}) collective-permute-start(bf16[24,128,128]{2,1,0:T(8,128)(2,1)S(1)} %get-tuple-element.128), channel_id=1, source_target_pairs={{0,128},{128,0},{1,129},{129,1},{2,130},{130,2},{3,131},{131,3},{4... | collective-permute-start | bytes 2359304 | tf_op jit(solution)/shard_map/ppermute | solution.py:33
  152.9 12.4 %collective-permute-start.35 = (bf16[2,16,6144]{2,1,0:T(8,128)(2,1)S(1)}, bf16[2,16,6144]{2,1,0:T(8,128)(2,1)S(1)}, u32[]{:S(2)}, u32[]{:S(2)}) collective-permute-start(bf16[2,16,6144]{2,1,0:T(8,128)(2,1)S(1)} %get-tuple-element.120), channel_id=1, source_target_pairs={{0,14},{2,0},{4,2},{6,4},{8,6},{10,8},{12,10},{14,12},{1,15},{3,1}... | collective-permute-start | bytes 1179656 | tf_op jit(solution)/shard_map/ppermute | solution.py:28
  155.1 10.1 %collective-permute-start.34 = (bf16[2,16,6144]{2,1,0:T(8,128)(2,1)S(1)}, bf16[2,16,6144]{2,1,0:T(8,128)(2,1)S(1)}, u32[]{:S(2)}, u32[]{:S(2)}) collective-permute-start(bf16[2,16,6144]{2,1,0:T(8,128)(2,1)S(1)} %get-tuple-element.121), channel_id=1, source_target_pairs={{0,2},{2,4},{4,6},{6,8},{8,10},{10,12},{12,14},{14,0},{1,3},{3,5},... | collective-permute-start | bytes 1179656 | tf_op jit(solution)/shard_map/ppermute | solution.py:28
  155.8 9.5 %collective-permute-start.36 = (f32[12288]{0:T(1024)S(1)}, f32[12288]{0:T(1024)S(1)}, u32[]{:S(2)}, u32[]{:S(2)}) collective-permute-start(f32[12288]{0:T(1024)S(1)} %slice_add_fusion.1), channel_id=1, source_target_pairs={{0,2},{2,0},{4,6},{6,4},{8,10},{10,8},{12,14},{14,12},{1,3},{3,1},... | collective-permute-start | bytes 147464 | tf_op jit(solution)/shard_map/ppermute | solution.py:33
  167.2 9.0 %copy-start.15 = (bf16[24,128,128]{2,1,0:T(8,128)(2,1)S(1)}, bf16[24,128,128]{2,1,0:T(8,128)(2,1)}, u32[]{:S(2)}) copy-start(bf16[24,128,128]{2,1,0:T(8,128)(2,1)} %get-tuple-element.101) | copy-start | bytes 2359300
  168.7 11.3 %collective-permute-start.40 = (bf16[2,16,6144]{2,1,0:T(8,128)(2,1)S(1)}, bf16[2,16,6144]{2,1,0:T(8,128)(2,1)S(1)}, u32[]{:S(2)}, u32[]{:S(2)}) collective-permute-start(bf16[2,16,6144]{2,1,0:T(8,128)(2,1)S(1)} %get-tuple-element.118), channel_id=1, source_target_pairs={{0,14},{2,0},{4,2},{6,4},{8,6},{10,8},{12,10},{14,12},{1,15},{3,1}... | collective-permute-start | bytes 1179656 | tf_op jit(solution)/shard_map/ppermute | solution.py:28
  171.0 9.1 %collective-permute-start.39 = (bf16[2,16,6144]{2,1,0:T(8,128)(2,1)S(1)}, bf16[2,16,6144]{2,1,0:T(8,128)(2,1)S(1)}, u32[]{:S(2)}, u32[]{:S(2)}) collective-permute-start(bf16[2,16,6144]{2,1,0:T(8,128)(2,1)S(1)} %get-tuple-element.119), channel_id=1, source_target_pairs={{0,2},{2,4},{4,6},{6,8},{8,10},{10,12},{12,14},{14,0},{1,3},{3,5},... | collective-permute-start | bytes 1179656 | tf_op jit(solution)/shard_map/ppermute | solution.py:28
  171.6 8.5 %collective-permute-start.41 = (f32[12288]{0:T(1024)S(1)}, f32[12288]{0:T(1024)S(1)}, u32[]{:S(2)}, u32[]{:S(2)}) collective-permute-start(f32[12288]{0:T(1024)S(1)} %add.207), channel_id=1, source_target_pairs={{0,4},{2,6},{4,0},{6,2},{8,12},{10,14},{12,8},{14,10},{1,5},{3,7},... | collective-permute-start | bytes 147464 | tf_op jit(solution)/shard_map/ppermute | solution.py:33
  176.7 21.4 %collective-permute-start.44 = (bf16[24,128,128]{2,1,0:T(8,128)(2,1)S(1)}, bf16[24,128,128]{2,1,0:T(8,128)(2,1)S(1)}, u32[]{:S(2)}, u32[]{:S(2)}) collective-permute-start(bf16[24,128,128]{2,1,0:T(8,128)(2,1)S(1)} %add_convert_fusion), channel_id=1, source_target_pairs={{0,64},{32,96},{64,0},{96,32},{1,65},{33,97},{65,1},{97,33},{2,66}... | collective-permute-start | bytes 2359304 | tf_op jit(solution)/shard_map/ppermute | solution.py:33
  176.8 21.3 %collective-permute-start.45 = (bf16[24,128,128]{2,1,0:T(8,128)(2,1)S(1)}, bf16[24,128,128]{2,1,0:T(8,128)(2,1)S(1)}, u32[]{:S(2)}, u32[]{:S(2)}) collective-permute-start(bf16[24,128,128]{2,1,0:T(8,128)(2,1)S(1)} %get-tuple-element.104), channel_id=1, source_target_pairs={{0,128},{128,0},{1,129},{129,1},{2,130},{130,2},{3,131},{131,3},{4... | collective-permute-start | bytes 2359304 | tf_op jit(solution)/shard_map/ppermute | solution.py:33
  181.2 22.6 %copy-start.12 = (bf16[24,128,128]{2,1,0:T(8,128)(2,1)S(1)}, bf16[24,128,128]{2,1,0:T(8,128)(2,1)}, u32[]{:S(2)}) copy-start(bf16[24,128,128]{2,1,0:T(8,128)(2,1)} %get-tuple-element.107) | copy-start | bytes 2359300
  181.3 16.8 %collective-permute-start.42 = (bf16[2,8,6144]{2,1,0:T(8,128)(2,1)S(1)}, bf16[2,8,6144]{2,1,0:T(8,128)(2,1)S(1)}, u32[]{:S(2)}, u32[]{:S(2)}) collective-permute-start(bf16[2,8,6144]{2,1,0:T(8,128)(2,1)S(1)} %slice.234), channel_id=1, source_target_pairs={{0,16},{16,0},{1,17},{17,1},{2,18},{18,2},{3,19},{19,3},{4,20},{20... | collective-permute-start | bytes 589832 | tf_op jit(solution)/shard_map/ppermute | solution.py:33
  182.7 6.8 %collective-permute-start.43 = (f32[12288]{0:T(1024)S(1)}, f32[12288]{0:T(1024)S(1)}, u32[]{:S(2)}, u32[]{:S(2)}) collective-permute-start(f32[12288]{0:T(1024)S(1)} %add.210), channel_id=1, source_target_pairs={{0,8},{2,10},{4,12},{6,14},{8,0},{10,2},{12,4},{14,6},{1,9},{3,11}... | collective-permute-start | bytes 147464 | tf_op jit(solution)/shard_map/ppermute | solution.py:33
  198.1 7.6 %collective-permute-start.47 = (f32[12288]{0:T(1024)S(1)}, f32[12288]{0:T(1024)S(1)}, u32[]{:S(2)}, u32[]{:S(2)}) collective-permute-start(f32[12288]{0:T(1024)S(1)} %add.216), channel_id=1, source_target_pairs={{0,1},{1,0},{2,3},{3,2},{4,5},{5,4},{6,7},{7,6},{8,9},{9,8},{10,11... | collective-permute-start | bytes 147464 | tf_op jit(solution)/shard_map/ppermute | solution.py:33
  203.7 2.7 %collective-permute-start.46 = (bf16[2,4,6144]{2,1,0:T(4,128)(2,1)S(1)}, bf16[2,4,6144]{2,1,0:T(4,128)(2,1)S(1)}, u32[]{:S(2)}, u32[]{:S(2)}) collective-permute-start(bf16[2,4,6144]{2,1,0:T(4,128)(2,1)S(1)} %select_convert_fusion), channel_id=1, source_target_pairs={{0,1},{1,0},{2,3},{3,2},{4,5},{5,4},{6,7},{7,6},{8,9},{9,8},{10,11... | collective-permute-start | bytes 294920 | tf_op jit(solution)/shard_map/ppermute | solution.py:33
  (12 other events, 41.2 us)
